TPU v7x, 32 devices: a whole 2x2x4 slice. The times are simulated.
32 devices in a mesh: clip: 16 (over z, x, core), tm: 2 (over y).
Axes of the slice: x: 2, y: 2, z: 4, core: 2. Of those that a mesh axis runs over, the one named last changes fastest.
Arguments:
- inputs: float32 [32, 2048, 512], P('clip', 'tm'), may hold values from -6 to 6
- band_ids: int32 [32], P('clip'), may hold values from 0 to 3
- offsets: int32 [32], P('clip'), may hold values from 0 to 511
- conv_weight: float32 [7, 512], replicated, may hold values from -2 to 2
- conv_bias: float32 [512], replicated, may hold values from -3 to 3
- scale_table: float32 [4, 512], replicated, may hold values from 0.25 to 1.75
- shift_table: float32 [4, 512], replicated, may hold values from -3 to 3
- up_weight: float32 [512, 1536], replicated, may hold values from -0.25 to 0.25
- up_bias: float32 [1536], replicated, may hold values from -3 to 3
- down_weight: float32 [1536, 512], replicated, may hold values from -0.15625 to 0.15625
- down_bias: float32 [512], replicated, may hold values from -2 to 2
- layer_scale: float32 [512], replicated, may hold values from 0.25 to 1.75
- head_weight: float32 [512, 1282], replicated, may hold values from -0.1875 to 0.1875
- head_bias: float32 [1282], replicated, may hold values from 1.5 to 3.5
- wave_cotangent: float32 [32, 655360], P('clip', 'tm'), may hold values from -6 to 6
Outputs:
- waveform: float32 [32, 655360], P('clip', 'tm')
- grad_inputs: float32 [32, 2048, 512], P('clip', 'tm')
- grad_conv_weight: float32 [7, 512], replicated
- grad_conv_bias: float32 [512], replicated
- grad_scale_table: float32 [4, 512], replicated
- grad_shift_table: float32 [4, 512], replicated
- grad_up_weight: float32 [512, 1536], replicated
- grad_up_bias: float32 [1536], replicated
- grad_down_weight: float32 [1536, 512], replicated
- grad_down_bias: float32 [512], replicated
- grad_layer_scale: float32 [512], replicated
- grad_head_weight: float32 [512, 1282], replicated
- grad_head_bias: float32 [1282], replicated
All inputs are finite; a program needn't handle non-finite values.
Results may differ from a plain program's by a relative error of at most 0.0003.
Values sent between devices are 32-bit elements; how exact they have to be, the bound alone decides.
No kernel may reach another device: no remote copies, remote signals or barrier semaphores. Data moves between devices by JAX's collectives and lax.ppermute only.
A program may use at most 192 MiB of HBM per device.

v0:
```python
import jax
import jax.numpy as jnp
from jax import lax
from jax.sharding import PartitionSpec as P

KERNEL = 7


def with_halo(value, sides, width):
    for axis, dim in sides:
        devices, length = (lax.axis_size(axis), value.shape[dim])
        up = [(i, (i + 1) % devices) for i in range(devices - 1)]
        down = [(j, i) for i, j in up]
        last = lax.slice_in_dim(value, length - width, length, axis=dim)
        initial = lax.slice_in_dim(value, 0, width, axis=dim)
        before = lax.ppermute(last, axis, up)
        after = lax.ppermute(initial, axis, down)
        value = jnp.concatenate([before, value, after], axis=dim)
    return value


def from_behind(block, axis, distance):
    devices = range(lax.axis_size(axis))
    route = [(i - distance, i) for i in devices if i - distance in devices]
    return lax.ppermute(block, axis, route)


def synthesis_table(fft_size, bin_count):
    highest_bin = bin_count - 1
    bin_index = jnp.arange(bin_count)
    sample_index = jnp.arange(fft_size)
    residue = bin_index[:, None] * sample_index[None, :] % fft_size
    angle_table = 2.0 * jnp.pi * residue.astype(jnp.float32) / fft_size
    edge_bin = (bin_index == 0) | (bin_index == highest_bin)
    factor = jnp.where(edge_bin, 1.0 / fft_size, 2.0 / fft_size).astype(jnp.float32)
    window = 0.5 - 0.5 * jnp.cos(2.0 * jnp.pi * sample_index.astype(jnp.float32) / fft_size)
    real_rows = factor[:, None] * jnp.cos(angle_table) * window[None, :]
    imag_rows = -factor[:, None] * jnp.sin(angle_table) * window[None, :]
    return (jnp.concatenate([real_rows, imag_rows], axis=0), window)


def body(
    inputs,
    band_ids,
    offsets,
    conv_weight,
    conv_bias,
    scale_table,
    shift_table,
    up_weight,
    up_bias,
    down_weight,
    down_bias,
    layer_scale,
    head_weight,
    head_bias,
    wave_cotangent,
):
    highest = lax.Precision.HIGHEST
    clip_count, frames, feature_count = inputs.shape
    fft_size = head_weight.shape[1] - 2
    bin_count = fft_size // 2 + 1
    hop_size = wave_cotangent.shape[1] // frames
    row_count = clip_count * frames
    start_frame = lax.axis_index("tm") * frames
    positions = start_frame + jnp.arange(frames)
    present = (positions[None, :] >= offsets[:, None]).astype(jnp.float32)
    masked = inputs * present[:, :, None]
    padded = with_halo(masked, (("tm", 1),), 3)
    conved = conv_bias + sum(
        (
            padded[:, kernel_pos : kernel_pos + frames] * conv_weight[kernel_pos]
            for kernel_pos in range(KERNEL)
        )
    )
    center = conved - jnp.mean(conved, axis=-1, keepdims=True)
    variance = jnp.mean(center * center, axis=-1, keepdims=True)
    inverse_std = lax.rsqrt(variance + 1e-06)
    normed = center * inverse_std
    onehot = (band_ids[:, None] == jnp.arange(scale_table.shape[0])[None, :]).astype(jnp.float32)
    scales = jnp.dot(onehot, scale_table, precision=highest)
    shifts = jnp.dot(onehot, shift_table, precision=highest)
    adapted = (normed * scales[:, None, :] + shifts[:, None, :]).reshape(row_count, feature_count)
    upward = jnp.dot(adapted, up_weight, precision=highest) + up_bias
    activated = jax.nn.gelu(upward, approximate=False)
    branch = jnp.dot(activated, down_weight, precision=highest) + down_bias
    residual_out = masked.reshape(row_count, feature_count) + layer_scale * branch
    logits = jnp.dot(residual_out, head_weight, precision=highest) + head_bias
    present_rows = present.reshape(row_count, 1)
    raw_mag = jnp.exp(logits[:, :bin_count])
    squashed = jnp.tanh(raw_mag / 100.0)
    magnitude = 100.0 * squashed * present_rows
    mag_slope = raw_mag * (1.0 - squashed * squashed) * present_rows
    angles = logits[:, bin_count:]
    cosine = jnp.cos(angles)
    sine_part = jnp.sin(angles)
    spectrum = jnp.concatenate([magnitude * cosine, magnitude * sine_part], axis=1)
    synthesis, window = synthesis_table(fft_size, bin_count)
    segments = jnp.dot(spectrum, synthesis, precision=highest).reshape(
        clip_count, frames, 4, hop_size
    )
    extended = sum(
        (
            jnp.pad(segments[:, :, quarter], ((0, 0), (quarter, 3 - quarter), (0, 0)))
            for quarter in range(4)
        )
    )
    wave_tail = extended[:, frames:].reshape(clip_count, 3 * hop_size)
    arrived = from_behind(wave_tail, "tm", 1).reshape(clip_count, 3, hop_size)
    summed = extended[:, :frames] + jnp.pad(arrived, ((0, 0), (0, frames - 3), (0, 0)))
    squares = (window * window).reshape(4, hop_size)
    envelope = sum(
        (
            ((positions - quarter)[None, :] >= offsets[:, None]).astype(jnp.float32)[:, :, None]
            * squares[quarter]
            for quarter in range(4)
        )
    )
    envelope = jnp.maximum(envelope, 1.0)
    waveform = (summed / envelope).reshape(clip_count, frames * hop_size)
    grad_summed = wave_cotangent.reshape(clip_count, frames, hop_size) / envelope
    returned = from_behind(grad_summed[:, :3].reshape(clip_count, 3 * hop_size), "tm", -1)
    grad_extended = jnp.concatenate(
        [grad_summed, returned.reshape(clip_count, 3, hop_size)], axis=1
    )
    grad_segments = jnp.stack(
        [grad_extended[:, quarter : quarter + frames] for quarter in range(4)], axis=2
    )
    grad_segments = grad_segments.reshape(row_count, fft_size)
    grad_spectrum = lax.dot_general(
        grad_segments, synthesis, (((1,), (1,)), ((), ())), precision=highest
    )
    grad_real = grad_spectrum[:, :bin_count]
    grad_imag = grad_spectrum[:, bin_count:]
    grad_logmag = mag_slope * (grad_real * cosine + grad_imag * sine_part)
    grad_angles = magnitude * (grad_imag * cosine - grad_real * sine_part)
    grad_logits = jnp.concatenate([grad_logmag, grad_angles], axis=1)
    grad_head_weight = lax.dot_general(
        residual_out, grad_logits, (((0,), (0,)), ((), ())), precision=highest
    )
    grad_head_bias = jnp.sum(grad_logits, axis=0)
    grad_mixed = lax.dot_general(
        grad_logits, head_weight, (((1,), (1,)), ((), ())), precision=highest
    )
    grad_layer_scale = jnp.sum(grad_mixed * branch, axis=0)
    grad_branch = grad_mixed * layer_scale
    grad_down_weight = lax.dot_general(
        activated, grad_branch, (((0,), (0,)), ((), ())), precision=highest
    )
    grad_down_bias = jnp.sum(grad_branch, axis=0)
    grad_activated = lax.dot_general(
        grad_branch, down_weight, (((1,), (1,)), ((), ())), precision=highest
    )
    normal_cdf = 0.5 * (1.0 + lax.erf(upward * 0.7071067811865476))
    density = jnp.exp(-0.5 * upward * upward) * 0.3989422804014327
    grad_upward = grad_activated * (normal_cdf + upward * density)
    grad_up_weight = lax.dot_general(
        adapted, grad_upward, (((0,), (0,)), ((), ())), precision=highest
    )
    grad_up_bias = jnp.sum(grad_upward, axis=0)
    grad_adapted = lax.dot_general(
        grad_upward, up_weight, (((1,), (1,)), ((), ())), precision=highest
    )
    grad_adapted = grad_adapted.reshape(clip_count, frames, feature_count)
    clip_scale_grads = jnp.sum(grad_adapted * normed, axis=1)
    clip_shift_grads = jnp.sum(grad_adapted, axis=1)
    grad_scale_table = lax.dot_general(
        onehot, clip_scale_grads, (((0,), (0,)), ((), ())), precision=highest
    )
    grad_shift_table = lax.dot_general(
        onehot, clip_shift_grads, (((0,), (0,)), ((), ())), precision=highest
    )
    grad_normed = grad_adapted * scales[:, None, :]
    grad_conved = inverse_std * (
        grad_normed
        - jnp.mean(grad_normed, axis=-1, keepdims=True)
        - normed * jnp.mean(grad_normed * normed, axis=-1, keepdims=True)
    )
    grad_conv_bias = jnp.sum(grad_conved, axis=(0, 1))
    grad_conv_weight = jnp.stack(
        [
            jnp.sum(padded[:, kernel_pos : kernel_pos + frames] * grad_conved, axis=(0, 1))
            for kernel_pos in range(KERNEL)
        ],
        axis=0,
    )
    grad_edges = with_halo(grad_conved, (("tm", 1),), 3)
    grad_masked = grad_mixed.reshape(clip_count, frames, feature_count) + sum(
        (
            conv_weight[kernel_pos] * grad_edges[:, 6 - kernel_pos : 6 - kernel_pos + frames]
            for kernel_pos in range(KERNEL)
        )
    )
    grad_inputs = grad_masked * present[:, :, None]
    (
        grad_conv_weight,
        grad_conv_bias,
        grad_scale_table,
        grad_shift_table,
        grad_up_weight,
        grad_up_bias,
        grad_down_weight,
        grad_down_bias,
        grad_layer_scale,
        grad_head_weight,
        grad_head_bias,
    ) = lax.psum(
        (
            grad_conv_weight,
            grad_conv_bias,
            grad_scale_table,
            grad_shift_table,
            grad_up_weight,
            grad_up_bias,
            grad_down_weight,
            grad_down_bias,
            grad_layer_scale,
            grad_head_weight,
            grad_head_bias,
        ),
        ("clip", "tm"),
    )
    return (
        waveform,
        grad_inputs,
        grad_conv_weight,
        grad_conv_bias,
        grad_scale_table,
        grad_shift_table,
        grad_up_weight,
        grad_up_bias,
        grad_down_weight,
        grad_down_bias,
        grad_layer_scale,
        grad_head_weight,
        grad_head_bias,
    )


def solution(mesh):
    in_specs = (
        P("clip", "tm", None),
        P("clip"),
        P("clip"),
        P(),
        P(),
        P(),
        P(),
        P(),
        P(),
        P(),
        P(),
        P(),
        P(),
        P(),
        P("clip", "tm"),
    )
    out_specs = (
        P("clip", "tm"),
        P("clip", "tm", None),
        P(),
        P(),
        P(),
        P(),
        P(),
        P(),
        P(),
        P(),
        P(),
        P(),
        P(),
    )
    return jax.shard_map(body, mesh=mesh, in_specs=in_specs, out_specs=out_specs, check_vma=False)
```

profile of v0, /device:TPU:0, one launch (start us, length us, event | category | flops | bytes accessed | tf_op | source)
XLA Modules:
  0.0 719.9 jit_solution(5819367147516743917)
XLA Ops:
  7.4 5.9 reshape.324
  13.3 3.4 copy.51
  17.4 2.8 fusion.67
  20.2 1.5 copy-done.15
  22.0 1.4 collective-permute-start.3
  23.4 2.5 broadcast_multiply_fusion
  26.0 2.0 copy-done.2
  28.6 4.9 collective-permute-start
  34.9 5.8 reshape.323
  41.3 3.6 copy.50
  45.0 4.3 fusion.66
  49.5 15.0 %multiply_multiply_fusion.7 = (f32[641,1280]{1,0:T(8,128)}, f32[641,1280]{1,0:T(8,128)}) fusion(f32[1280]{0:T(1024)S(1)} %multiply_subtract_fusion, f32[641]{0:T(1024)S(1)} %get-tuple-element.89, f32[641]{0:T(1024)S(1)} %get-tuple-element.90), kind=kLoop, calls=%fused_computation.108 | loop fusion | flops 10666240 | bytes 6574088 | tf_op jit(solution)/shard_map/mul | solution.py:37
  66.1 6.9 fusion.59
  73.0 2.3 pad_maximum_fusion.1
  75.3 10.4 %copy.54 = f32[2,1024,4,320]{1,0,3,2:T(2,128)S(1)} copy(f32[2,1024,4,320]{1,3,0,2:T(8,128)S(1)} %pad_maximum_fusion.1) | data formatting | bytes 20971520 | tf_op jit(solution)/shard_map/stack | solution.py:126
  85.7 9.2 %copy.61 = f32[160,8,2,1024]{3,1,2,0:T(8,128)} copy(f32[160,8,2,1024]{3,2,1,0:T(2,128)S(1)} %bitcast.93) | data formatting | bytes 20971520
  95.0 53.9 %fusion.21 = f32[2048,1282]{0,1:T(8,128)} fusion(f32[2048,1280]{0,1:T(8,128)} %bitcast.102, f32[641,1280]{1,0:T(8,128)} %get-tuple-element.70, f32[641,1280]{1,0:T(8,128)} %get-tuple-element.69), kind=kOutput, calls=%fused_computation.43 | convolution fusion | flops 40329875456 | bytes 27551744 | tf_op jit(solution)/shard_map/dot_general | solution.py:130
  149.0 4.5 fusion.91
  155.6 48.0 %fusion.1 = (f32[2048,1536]{1,0:T(8,128)S(1)}, f32[2048,1536]{1,0:T(8,128)}) fusion(f32[1536]{0:T(1024)S(1)} %copy-done.82, f32[2048,512]{1,0:T(8,128)S(1)} %bitcast.104, f32[512,1536]{1,0:T(8,128)S(1)} %copy-done), kind=kOutput, calls=%fused_computation.3 | convolution fusion | flops 19531825152 | bytes 32512000 | tf_op jit(solution)/shard_map/dot_general | solution.py:84
  203.6 20.8 %bitcast_add_fusion = (f32[2048,512]{1,0:T(8,128)S(1)}, f32[2048,512]{1,0:T(8,128)S(1)}) fusion(f32[2,1024,512]{2,1,0:T(8,128)S(1)} %copy-done.3, f32[512]{0:T(512)S(1)} %copy-done.72, f32[512]{0:T(512)S(1)} %copy-done.73, f32[2048,1536]{1,0:T(8,128)S(1)} %get-tuple-element.76, f32[1536,512]{1,0:T(8,128)S(1)} %copy-done.24), kind=kOutput, calls=%fused_computation.81 | convolution fusion | flops 19330498560 | bytes 28315648 | tf_op jit(solution)/shard_map/dot_general | solution.py:86
  224.5 21.2 %convolution_add_fusion = f32[2048,1282]{0,1:T(8,128)} fusion(f32[2048,512]{1,0:T(8,128)S(1)} %get-tuple-element.78, f32[512,1282]{0,1:T(8,128)} %param.27, f32[1282]{0:T(1024)S(1)} %copy-done.81), kind=kOutput, calls=%fused_computation.30 | convolution fusion | flops 16133918720 | bytes 17327112 | tf_op jit(solution)/shard_map/dot_general | solution.py:88
  245.8 26.2 %add_multiply_fusion = (f32[2048,641]{0,1:T(8,128)S(1)}, f32[2048,641]{0,1:T(8,128)S(1)}, f32[2048,641]{0,1:T(8,128)}, f32[2048,641]{0,1:T(8,128)}) fusion(f32[2048,1282]{0,1:T(8,128)} %fusion.21, f32[2048,1282]{0,1:T(8,128)} %convolution_add_fusion, f32[2048]{0:T(1024)S(1)} %bitcast.107, f32[2048]{0:T(1024)S(1)} %bitcast.106), kind=kLoop, calls=%fused_computation.46 | loop fusion | flops 21004288 | bytes 42024960 | tf_op jit(solution)/shard_map/mul | solution.py:135
  272.0 22.9 %fusion.19 = f32[512,1282]{0,1:T(8,128)} fusion(f32[2048,512]{1,0:T(8,128)S(1)} %copy-done.18, f32[2048,641]{0,1:T(8,128)S(1)} %get-tuple-element.44, f32[2048,641]{0,1:T(8,128)S(1)} %get-tuple-element.43), kind=kOutput, calls=%fused_computation.32 | convolution fusion | flops 16133918720 | bytes 17321984 | tf_op jit(solution)/shard_map/dot_general | solution.py:138
  294.9 24.6 %multiply_reduce_fusion = (f32[512]{0:T(512)S(1)}, f32[512]{0:T(512)}, f32[2048,512]{1,0:T(8,128)S(1)}) fusion(f32[2048,512]{1,0:T(8,128)S(1)} %get-tuple-element.79, f32[512]{0:T(512)S(1)} %copy-done.72, f32[512]{0:T(512)S(1)} %copy-done.73, f32[512,1282]{0,1:T(8,128)} %param.27, f32[2048,641]{0,1:T(8,128)S(1)} %get-tuple-element.44, ...), kind=kOutput, calls=%fused_computation.82 | convolution fusion | flops 16139160576 | bytes 21524480 | tf_op jit(solution)/shard_map/dot_general | solution.py:142
  319.4 23.1 %fusion.48 = f32[1536,512]{1,0:T(8,128)} fusion(f32[2048,1536]{1,0:T(8,128)S(1)} %get-tuple-element.76, f32[2048,512]{1,0:T(8,128)S(1)} %get-tuple-element.84, f32[512]{0:T(512)S(1)} %copy-done.73), kind=kOutput, calls=%fused_computation.102 | convolution fusion | flops 19328401408 | bytes 19924992 | tf_op jit(solution)/shard_map/dot_general | solution.py:147
  342.5 30.2 %fusion.97 = (f32[1536]{0:T(1024)}, f32[2048,1536]{1,0:T(8,128)S(1)}) fusion(f32[2048,1536]{1,0:T(8,128)} %get-tuple-element.77, f32[1536]{0:T(1024)S(1)} %copy-done.82, f32[1536,512]{1,0:T(8,128)} %param.24, f32[2048,512]{1,0:T(8,128)S(1)} %get-tuple-element.84, f32[512]{0:T(512)S(1)} %copy-done.73), kind=kOutput, calls=%fused_computation.183 | convolution fusion | flops 19363002368 | bytes 32520192 | tf_op jit(solution)/shard_map/dot_general | solution.py:151
  372.7 4.6 copy-done.14
  377.3 22.8 %fusion.98 = f32[512,1536]{1,0:T(8,128)} fusion(f32[2048,512]{1,0:T(8,128)S(1)} %bitcast.105, f32[2048,1536]{1,0:T(8,128)S(1)} %get-tuple-element.83), kind=kOutput, calls=%fused_computation.184 | convolution fusion | flops 19327352832 | bytes 19922944 | tf_op jit(solution)/shard_map/dot_general | solution.py:157
  400.1 24.1 %fusion.45 = (f32[2048]{0:T(1024)S(1)}, f32[2048,512]{1,0:T(8,128)}) fusion(f32[2,512]{1,0:T(2,128)S(1)} %copy-done.44, f32[2048,1536]{1,0:T(8,128)} %copy-done.14, f32[512,1536]{1,0:T(8,128)S(1)} %copy-done), kind=kOutput, calls=%fused_computation.79 | convolution fusion | flops 19329447936 | bytes 19935232 | tf_op jit(solution)/shard_map/dot_general | solution.py:161
  424.1 54.2 %fusion.14 = f32[2048,1280]{0,1:T(8,128)} fusion(f32[2048,641]{0,1:T(8,128)} %get-tuple-element.45, f32[2048,641]{0,1:T(8,128)} %get-tuple-element.46, f32[641,1280]{1,0:T(8,128)S(1)} %copy-done.23, f32[641,1280]{1,0:T(8,128)S(1)} %copy-done.22), kind=kOutput, calls=%fused_computation.24 | convolution fusion | flops 40332500992 | bytes 27551744 | tf_op jit(solution)/shard_map/dot_general | solution.py:99
  478.3 14.3 %reshape.319 = f32[2,1024,4,320]{1,0,3,2:T(2,128)} reshape(f32[2048,1280]{0,1:T(8,128)} %fusion.14) | data formatting | bytes 20971520 | tf_op jit(solution)/shard_map/reshape | solution.py:99
  492.6 6.6 fusion.92
  504.7 4.5 collective-permute-start.2
  509.3 5.9 multiply_reduce_fusion.1
  516.2 19.7 %multiply_reduce_fusion.2 = (f32[512]{0:T(512)S(1)}, f32[512]{0:T(512)S(1)}, f32[512]{0:T(512)S(1)}, f32[512]{0:T(512)S(1)}, f32[512]{0:T(512)S(1)}, /*index=5*/...) fusion(f32[2,3,512]{2,1,0:T(4,128)S(1)} %copy-done.42, f32[2,1024,512]{2,1,0:T(8,128)} %copy-done.2, ...), kind=kLoop, calls=%fused_computation.84 | loop fusion | flops 29356032 | bytes 16855040 | tf_op jit(solution)/shard_map/reduce_sum | solution.py:182
  535.9 1.9 copy-done.13
  538.5 5.3 fusion.18
  545.5 5.8 pad_add_fusion
  552.8 5.1 collective-permute-start.5
  558.0 43.1 %all-reduce.5 = (f32[7,512]{1,0:T(8,128)}, f32[512]{0:T(512)}, f32[4,512]{1,0:T(4,128)}, f32[4,512]{1,0:T(4,128)}, f32[1536]{0:T(1024)}, /*index=5*/f32[512]{0:T(512)}, f32[512]{0:T(512)}, f32[1282]{0:T(1024)}) all-reduce(f32[7,512]{1,0:T(8,128)S(1)} %stack.48, ...), channel_id=1, replica_groups=mesh['clip'=16,'tm'=2] {'clip','tm'}, use_global_device_ids=true, to_apply=%region_11.12 | all-reduce | flops 12034 | bytes 96272 | tf_op jit(solution)/shard_map/psum | solution.py:207
  601.5 4.3 fusion.61
  605.8 3.5 copy.48
  609.3 6.0 reshape.322
  615.4 16.6 %fusion.28 = f32[2,1024,512]{2,1,0:T(8,128)} fusion(f32[2,1024,512]{2,1,0:T(8,128)} %bitcast.103, f32[2,3,512]{2,1,0:T(4,128)} %collective-permute-done.5, f32[2,3,512]{2,1,0:T(4,128)S(1)} %collective-permute-done.4, f32[2,1024,512]{2,1,0:T(8,128)} %copy-done.13, f32[512]{0:T(512)S(1)} %bitcast.119, f32[512]{0:T(512)S(1)} %bitcast.121, f32[512]{0:T(512)S(1)} %bitcast.111, ...), kind=kLoop, calls=%fused_computation.57 | loop fusion | flops 22020096 | bytes 12630016 | tf_op jit(solution)/shard_map/mul | solution.py:194
  632.0 72.6 %all-reduce.9.cloned.1.call-done = (f32[512,1536]{1,0:T(8,128)}, f32[1536,512]{1,0:T(8,128)}, f32[512,1282]{0,1:T(8,128)}) async-done(((f32[512,1536]{1,0:T(8,128)}, f32[1536,512]{1,0:T(8,128)}, f32[512,1282]{0,1:T(8,128)}), (f32[512,1536]{1,0:T(8,128)}, f32[1536,512]{1,0:T(8,128)}, f32[512,1282]{0,1:T(8,128)})) %all-reduce.9.cloned.1.call-update) | async-done | bytes 8917008 | tf_op jit(solution)/shard_map/psum | solution.py:207
  704.5 3.9 copy.77
  708.5 1.7 copy.78
  711.3 1.5 copy.79
  (215 shorter events, 19.5 us)
Async XLA Ops:
  7.2 148.4 %copy-start = (f32[512,1536]{1,0:T(8,128)S(1)}, f32[512,1536]{1,0:T(8,128)}, u32[]{:S(2)}) copy-start(f32[512,1536]{1,0:T(8,128)} %param.22) | copy-start | bytes 9437188
  7.2 697.4 %all-reduce.9.cloned.1.call-start = ((), (), s32[]{:S(2)}) async-start(), calls=%async_computation | async-start | bytes 17858560 | tf_op jit(solution)/shard_map/psum | solution.py:207
  7.4 37.5 %copy-start.45 = (f32[320]{0:T(512)}, f32[320]{0:T(512)S(1)}, u32[]{:S(2)}) copy-start(f32[320]{0:T(512)S(1)} %get-tuple-element.65) | copy-start | bytes 3844
  7.4 37.5 %copy-start.47 = (f32[320]{0:T(512)}, f32[320]{0:T(512)S(1)}, u32[]{:S(2)}) copy-start(f32[320]{0:T(512)S(1)} %get-tuple-element.66) | copy-start | bytes 3844
  7.4 37.5 %copy-start.49 = (f32[320]{0:T(512)}, f32[320]{0:T(512)S(1)}, u32[]{:S(2)}) copy-start(f32[320]{0:T(512)S(1)} %get-tuple-element.67) | copy-start | bytes 3844
  17.4 27.5 %copy-start.27 = (f32[2,1024]{1,0:T(2,128)}, f32[2,1024]{1,0:T(2,128)S(1)}, u32[]{:S(2)}) copy-start(f32[2,1024]{1,0:T(2,128)S(1)} %get-tuple-element.72) | copy-start | bytes 24580
  17.4 27.5 %copy-start.31 = (f32[2,1024]{1,0:T(2,128)}, f32[2,1024]{1,0:T(2,128)S(1)}, u32[]{:S(2)}) copy-start(f32[2,1024]{1,0:T(2,128)S(1)} %get-tuple-element.73) | copy-start | bytes 24580
  17.4 27.5 %copy-start.33 = (f32[2,1024]{1,0:T(2,128)}, f32[2,1024]{1,0:T(2,128)S(1)}, u32[]{:S(2)}) copy-start(f32[2,1024]{1,0:T(2,128)S(1)} %get-tuple-element.74) | copy-start | bytes 24580
  17.4 27.5 %copy-start.35 = (f32[2,1024]{1,0:T(2,128)}, f32[2,1024]{1,0:T(2,128)S(1)}, u32[]{:S(2)}) copy-start(f32[2,1024]{1,0:T(2,128)S(1)} %get-tuple-element.75) | copy-start | bytes 24580
  22.0 43.8 %collective-permute-start.3 = (f32[2,960]{1,0:T(2,128)S(1)}, f32[2,960]{1,0:T(2,128)S(1)}, u32[]{:S(2)}, u32[]{:S(2)}) collective-permute-start(f32[2,960]{1,0:T(2,128)S(1)} %reshape.325), channel_id=1, source_target_pairs={{1,0},{3,2},{5,4},{7,6},{9,8},{11,10},{13,12},{15,14},{17,16},{19,... | collective-permute-start | bytes 23048 | tf_op jit(solution)/shard_map/ppermute | solution.py:25
  28.6 120.3 %collective-permute-start = (f32[2,3,512]{2,1,0:T(4,128)}, f32[2,3,512]{2,1,0:T(4,128)S(1)}, u32[]{:S(2)}, u32[]{:S(2)}) collective-permute-start(f32[2,3,512]{2,1,0:T(4,128)} %get-tuple-element.53), channel_id=1, source_target_pairs={{0,1},{2,3},{4,5},{6,7},{8,9},{10,11},{12,13},{14,15},{16,17},{18,... | collective-permute-start | bytes 36872 | tf_op jit(solution)/shard_map/ppermute | solution.py:16
  33.5 115.5 %collective-permute-start.1 = (f32[2,3,512]{2,1,0:T(4,128)}, f32[2,3,512]{2,1,0:T(4,128)S(1)}, u32[]{:S(2)}, u32[]{:S(2)}) collective-permute-start(f32[2,3,512]{2,1,0:T(4,128)} %get-tuple-element.54), channel_id=1, source_target_pairs={{1,0},{3,2},{5,4},{7,6},{9,8},{11,10},{13,12},{15,14},{17,16},{19,... | collective-permute-start | bytes 36872 | tf_op jit(solution)/shard_map/ppermute | solution.py:17
  49.5 105.0 %copy-start.43 = (f32[2,512]{1,0:T(2,128)}, f32[2,512]{1,0:T(2,128)S(1)}, u32[]{:S(2)}) copy-start(f32[2,512]{1,0:T(2,128)S(1)} %fusion.81) | copy-start | bytes 12292
  95.0 54.0 %copy-start.3 = (f32[2,1024,512]{2,1,0:T(8,128)S(1)}, f32[2,1024,512]{2,1,0:T(8,128)}, u32[]{:S(2)}) copy-start(f32[2,1024,512]{2,1,0:T(8,128)} %copy-done.2) | copy-start | bytes 12582916
  95.0 54.0 %copy-start.57 = (f32[1,512]{1,0:T(1,128)S(1)}, f32[1,512]{1,0:T(1,128)}, u32[]{:S(2)}) copy-start(f32[1,512]{1,0:T(1,128)} %get-tuple-element.58) | copy-start | bytes 6148
  95.0 54.0 %copy-start.59 = (f32[1,512]{1,0:T(1,128)S(1)}, f32[1,512]{1,0:T(1,128)}, u32[]{:S(2)}) copy-start(f32[1,512]{1,0:T(1,128)} %get-tuple-element.59) | copy-start | bytes 6148
  95.0 54.0 %copy-start.61 = (f32[1,512]{1,0:T(1,128)S(1)}, f32[1,512]{1,0:T(1,128)}, u32[]{:S(2)}) copy-start(f32[1,512]{1,0:T(1,128)} %get-tuple-element.60) | copy-start | bytes 6148
  95.0 54.0 %copy-start.63 = (f32[1,512]{1,0:T(1,128)S(1)}, f32[1,512]{1,0:T(1,128)}, u32[]{:S(2)}) copy-start(f32[1,512]{1,0:T(1,128)} %get-tuple-element.61) | copy-start | bytes 6148
  95.0 54.0 %copy-start.65 = (f32[1,512]{1,0:T(1,128)S(1)}, f32[1,512]{1,0:T(1,128)}, u32[]{:S(2)}) copy-start(f32[1,512]{1,0:T(1,128)} %get-tuple-element.62) | copy-start | bytes 6148
  95.0 54.0 %copy-start.67 = (f32[1,512]{1,0:T(1,128)S(1)}, f32[1,512]{1,0:T(1,128)}, u32[]{:S(2)}) copy-start(f32[1,512]{1,0:T(1,128)} %get-tuple-element.63) | copy-start | bytes 6148
  95.0 54.0 %copy-start.69 = (f32[1,512]{1,0:T(1,128)S(1)}, f32[1,512]{1,0:T(1,128)}, u32[]{:S(2)}) copy-start(f32[1,512]{1,0:T(1,128)} %get-tuple-element.64) | copy-start | bytes 6148
  95.0 54.0 %copy-start.75 = (f32[512]{0:T(512)S(1)}, f32[512]{0:T(512)}, u32[]{:S(2)}) copy-start(f32[512]{0:T(512)} %param.19) | copy-start | bytes 6148
  155.6 48.0 %copy-start.20 = (f32[2,1024,512]{2,1,0:T(8,128)}, f32[2,1024,512]{2,1,0:T(8,128)S(1)}, u32[]{:S(2)}) copy-start(f32[2,1024,512]{2,1,0:T(8,128)S(1)} %multiply_add_fusion) | copy-start | bytes 12582916
  155.6 48.0 %copy-start.24 = (f32[1536,512]{1,0:T(8,128)S(1)}, f32[1536,512]{1,0:T(8,128)}, u32[]{:S(2)}) copy-start(f32[1536,512]{1,0:T(8,128)} %param.24) | copy-start | bytes 9437188
  155.6 48.0 %copy-start.72 = (f32[512]{0:T(512)S(1)}, f32[512]{0:T(512)}, u32[]{:S(2)}) copy-start(f32[512]{0:T(512)} %param.25) | copy-start | bytes 6148
  155.6 48.0 %copy-start.73 = (f32[512]{0:T(512)S(1)}, f32[512]{0:T(512)}, u32[]{:S(2)}) copy-start(f32[512]{0:T(512)} %param.26) | copy-start | bytes 6148
  224.5 21.3 %copy-start.17 = (f32[2048,512]{1,0:T(8,128)}, f32[2048,512]{1,0:T(8,128)S(1)}, u32[]{:S(2)}) copy-start(f32[2048,512]{1,0:T(8,128)S(1)} %get-tuple-element.78) | copy-start | bytes 12582916
  224.5 21.3 %copy-start.54 = (f32[1,8,2,128]{3,1,2,0:T(8,128)S(1)}, f32[1,8,2,128]{3,1,2,0:T(8,128)}, u32[]{:S(2)}) copy-start(f32[1,8,2,128]{3,1,2,0:T(8,128)} %copy.73) | copy-start | bytes 24580
  224.5 21.3 %copy-start.55 = (f32[1,8,2,128]{3,1,2,0:T(8,128)S(1)}, f32[1,8,2,128]{3,1,2,0:T(8,128)}, u32[]{:S(2)}) copy-start(f32[1,8,2,128]{3,1,2,0:T(8,128)} %copy.72) | copy-start | bytes 24580
  245.8 26.2 %copy-start.18 = (f32[2048,512]{1,0:T(8,128)S(1)}, f32[2048,512]{1,0:T(8,128)}, u32[]{:S(2)}) copy-start(f32[2048,512]{1,0:T(8,128)} %copy-done.17) | copy-start | bytes 12582916
  272.0 22.9 %copy-start.11 = (f32[2048,641]{0,1:T(8,128)}, f32[2048,641]{0,1:T(8,128)S(1)}, u32[]{:S(2)}) copy-start(f32[2048,641]{0,1:T(8,128)S(1)} %get-tuple-element.43) | copy-start | bytes 15753220
  272.0 22.9 %copy-start.12 = (f32[2048,641]{0,1:T(8,128)}, f32[2048,641]{0,1:T(8,128)S(1)}, u32[]{:S(2)}) copy-start(f32[2048,641]{0,1:T(8,128)S(1)} %get-tuple-element.44) | copy-start | bytes 15753220
  319.4 23.1 %copy-start.19 = (f32[2048,512]{1,0:T(8,128)}, f32[2048,512]{1,0:T(8,128)S(1)}, u32[]{:S(2)}) copy-start(f32[2048,512]{1,0:T(8,128)S(1)} %get-tuple-element.84) | copy-start | bytes 12582916
  342.5 34.8 %copy-start.21 = (f32[2,1024,512]{2,1,0:T(8,128)S(1)}, f32[2,1024,512]{2,1,0:T(8,128)}, u32[]{:S(2)}) copy-start(f32[2,1024,512]{2,1,0:T(8,128)} %copy-done.20) | copy-start | bytes 12582916
  377.3 22.8 %copy-start.44 = (f32[2,512]{1,0:T(2,128)S(1)}, f32[2,512]{1,0:T(2,128)}, u32[]{:S(2)}) copy-start(f32[2,512]{1,0:T(2,128)} %copy-done.43) | copy-start | bytes 12292
  400.0 24.1 %copy-start.22 = (f32[641,1280]{1,0:T(8,128)S(1)}, f32[641,1280]{1,0:T(8,128)}, u32[]{:S(2)}) copy-start(f32[641,1280]{1,0:T(8,128)} %get-tuple-element.69) | copy-start | bytes 9845764
  400.0 24.1 %copy-start.23 = (f32[641,1280]{1,0:T(8,128)S(1)}, f32[641,1280]{1,0:T(8,128)}, u32[]{:S(2)}) copy-start(f32[641,1280]{1,0:T(8,128)} %get-tuple-element.70) | copy-start | bytes 9845764
  504.7 96.4 %collective-permute-start.2 = (f32[2,960]{1,0:T(2,128)S(1)}, f32[2,960]{1,0:T(2,128)S(1)}, u32[]{:S(2)}, u32[]{:S(2)}) collective-permute-start(f32[2,960]{1,0:T(2,128)S(1)} %reshape.320), channel_id=1, source_target_pairs={{0,1},{2,3},{4,5},{6,7},{8,9},{10,11},{12,13},{14,15},{16,17},{18,... | collective-permute-start | bytes 23048 | tf_op jit(solution)/shard_map/ppermute | solution.py:25
  545.4 56.0 %copy-start.28 = (f32[2,1024]{1,0:T(2,128)S(1)}, f32[2,1024]{1,0:T(2,128)}, u32[]{:S(2)}) copy-start(f32[2,1024]{1,0:T(2,128)} %copy-done.27) | copy-start | bytes 24580
  545.4 56.0 %copy-start.32 = (f32[2,1024]{1,0:T(2,128)S(1)}, f32[2,1024]{1,0:T(2,128)}, u32[]{:S(2)}) copy-start(f32[2,1024]{1,0:T(2,128)} %copy-done.31) | copy-start | bytes 24580
  545.4 56.0 %copy-start.34 = (f32[2,1024]{1,0:T(2,128)S(1)}, f32[2,1024]{1,0:T(2,128)}, u32[]{:S(2)}) copy-start(f32[2,1024]{1,0:T(2,128)} %copy-done.33) | copy-start | bytes 24580
  545.4 56.0 %copy-start.36 = (f32[2,1024]{1,0:T(2,128)S(1)}, f32[2,1024]{1,0:T(2,128)}, u32[]{:S(2)}) copy-start(f32[2,1024]{1,0:T(2,128)} %copy-done.35) | copy-start | bytes 24580
  545.4 56.0 %copy-start.46 = (f32[320]{0:T(512)S(1)}, f32[320]{0:T(512)}, u32[]{:S(2)}) copy-start(f32[320]{0:T(512)} %copy-done.45) | copy-start | bytes 3844
  545.4 56.0 %copy-start.48 = (f32[320]{0:T(512)S(1)}, f32[320]{0:T(512)}, u32[]{:S(2)}) copy-start(f32[320]{0:T(512)} %copy-done.47) | copy-start | bytes 3844
  545.4 56.0 %copy-start.50 = (f32[320]{0:T(512)S(1)}, f32[320]{0:T(512)}, u32[]{:S(2)}) copy-start(f32[320]{0:T(512)} %copy-done.49) | copy-start | bytes 3844
  545.5 56.0 %copy-start.53 = (f32[320]{0:T(512)S(1)}, f32[320]{0:T(512)}, u32[]{:S(2)}) copy-start(f32[320]{0:T(512)} %copy-done.51) | copy-start | bytes 3844
  551.5 63.8 %collective-permute-start.4 = (f32[2,3,512]{2,1,0:T(4,128)}, f32[2,3,512]{2,1,0:T(4,128)S(1)}, u32[]{:S(2)}, u32[]{:S(2)}) collective-permute-start(f32[2,3,512]{2,1,0:T(4,128)} %get-tuple-element.51), channel_id=1, source_target_pairs={{1,0},{3,2},{5,4},{7,6},{9,8},{11,10},{13,12},{15,14},{17,16},{19,... | collective-permute-start | bytes 36872 | tf_op jit(solution)/shard_map/ppermute | solution.py:17
  552.8 62.5 %collective-permute-start.5 = (f32[2,3,512]{2,1,0:T(4,128)}, f32[2,3,512]{2,1,0:T(4,128)}, u32[]{:S(2)}, u32[]{:S(2)}) collective-permute-start(f32[2,3,512]{2,1,0:T(4,128)} %get-tuple-element.52), channel_id=1, source_target_pairs={{0,1},{2,3},{4,5},{6,7},{8,9},{10,11},{12,13},{14,15},{16,17},{18,... | collective-permute-start | bytes 36872 | tf_op jit(solution)/shard_map/ppermute | solution.py:16
  (44 other events, 261.3 us)
Sparse Core Ops, SparseCore 0:
  515.7 188.8 all-reduce.8
where the time goes:
time: 726 us; the launch traced here: 720 us
  matrix products  347 us (48%)
  other arithmetic  125 us (17%)
  local copies, waits for them, and re-layouts  98.8 us (14%)
  waiting for transfers between devices  72.6 us (10%)
  blocking collectives  43.1 us (6%)
  starting transfers between devices  18.6 us (3%)
  between operations  15.3 us (2%)
    psum x1, waiting for transfers between devices, body(): lax.psum((grad_conv_weight, grad_conv_bias, grad_scale_table, grad_shift_...  72.6 us
    dot_general x1, matrix products, body(): jnp.dot(spectrum, synthesis, precision=highest)  54.2 us
    dot_general x1, matrix products, body(): lax.dot_general(grad_segments, synthesis, (((1,), (1,)), ((), ())), preci...  53.9 us
    dot_general x1, matrix products, body(): upward = jnp.dot(adapted, up_weight, precision=highest) + up_bias  48 us
    psum x1, blocking collectives, body(): lax.psum((grad_conv_weight, grad_conv_bias, grad_scale_table, grad_shift_...  43.1 us
    unnamed x179, local copies, waits for them, and re-layouts  35.5 us
    dot_general x1, matrix products, body(): lax.dot_general(grad_branch, down_weight, (((1,), (1,)), ((), ())), preci...  30.2 us
    mul x1, other arithmetic, body(): grad_logmag = mag_slope * (grad_real * cosine + grad_imag * sine_part)  26.2 us
  transfers between devices with their start and end apart: 7, of which 1 were waited for; matrix products, arithmetic and copies ran while one was open for 26% of the time, Pallas kernels for 0%

commit v1 on v0

v1 whole, which is shorter than its diff:
```python
import functools

import jax
import jax.numpy as jnp
import ml_dtypes
import numpy as np
from jax import lax
from jax.experimental import pallas as pl
from jax.experimental.pallas import tpu as pltpu
from jax.sharding import PartitionSpec as P

KERNEL = 7
F32 = jnp.float32
BF16 = jnp.bfloat16
LANES = 128
PAIRS = 128
ROWS = 2 * PAIRS
VMEM = 60 * 2**20
SDS = jax.ShapeDtypeStruct

SIN_POLY = (0.999999996, -0.166666580, 8.33305023e-03, -1.98090119e-04, 2.60507821e-06)
COS_POLY = (1.0, -0.499999994, 4.16666361e-02, -1.38883598e-03, 2.47600798e-05, -2.60500270e-07)

NN = (((1,), (0,)), ((), ()))
NT = (((1,), (1,)), ((), ()))


def split(x):
    high = x.astype(BF16)
    return high, (x - high.astype(F32)).astype(BF16)


def dot(a, b, dims=NN):
    return lax.dot_general(a, b, dims, preferred_element_type=F32)


def dot3(a, b, dims=NN):
    return dot(a[0], b[0], dims) + (dot(a[0], b[1], dims) + dot(a[1], b[0], dims))


def fold8(x):
    return jnp.sum(x.reshape(x.shape[0] // 8, 8, x.shape[1]), axis=0)


def np_split(x):
    high = x.astype(np.float32).astype(ml_dtypes.bfloat16)
    return high, (x - high.astype(np.float64)).astype(ml_dtypes.bfloat16)


@functools.lru_cache(None)
def tables(nfft):
    fifth, half, hop = nfft // 5, nfft // 2, nfft // 4
    bins = np.arange(1, half)
    first = bins[np.isin(bins % 5, (1, 4))]
    second = bins[np.isin(bins % 5, (2, 3))]
    zero = np.arange(0, half, 5)
    n0 = np.arange(fifth)

    def paired(ks, residue):
        sign = np.where(ks % 5 == residue, 1.0, -1.0)[:, None]
        turn = 2 * np.pi * ((sign * ks[:, None] * n0[None]) % nfft) / nfft
        weight = 2.0 / nfft
        real = np.concatenate([weight * np.cos(turn), weight * np.sin(turn)], 1)
        imag = np.concatenate([-sign * weight * np.sin(turn), sign * weight * np.cos(turn)], 1)
        return np.concatenate([real, imag], 0)

    turn = 2 * np.pi * ((zero[:, None] * n0[None]) % nfft) / nfft
    weight = np.where(zero == 0, 1.0, 2.0)[:, None] / nfft
    real, imag = weight * np.cos(turn), -weight * np.sin(turn)
    imag[0] = np.cos(np.pi * n0) / nfft
    transforms = [np_split(t) for t in (paired(first, 1), paired(second, 2), np.concatenate([real, imag], 0))]
    n = np.arange(nfft)
    window = 0.5 - 0.5 * np.cos(2 * np.pi * n / nfft)
    windows = np.stack([window, np.roll(window, hop)]).astype(np.float32)
    squares = np.cumsum((window**2).reshape(4, hop), axis=0)
    inverse = np.tile(1.0 / np.maximum(squares, 1.0), (1, 2)).astype(np.float32)
    order = np.concatenate([first, half + 1 + first, second, half + 1 + second, zero, half + 1 + zero])
    turns = np.zeros(nfft)
    place = 0
    for ks in (first, second, zero):
        turns[place + len(ks) : place + 2 * len(ks)] = -(np.pi / 2) * (ks % 4)
        place += 2 * len(ks)
    return transforms, windows, inverse, order, turns.astype(np.float32), (len(first), len(second), len(zero))


def sin_cos(x):
    turns = jnp.round(x * np.float32(0.5 / np.pi))
    h = x * 0.5 - turns * np.float32(3.140625)
    h = h - turns * np.float32(9.67502593994140625e-4)
    h = h - turns * np.float32(1.509957990978376432e-7)
    z = h * h
    s = np.float32(SIN_POLY[-1])
    for c in SIN_POLY[-2::-1]:
        s = s * z + np.float32(c)
    s = s * h
    cosine = np.float32(COS_POLY[-1])
    for c in COS_POLY[-2::-1]:
        cosine = cosine * z + np.float32(c)
    twice = s + s
    return twice * cosine, 1.0 - twice * s


def fifths():
    a = 2 * np.pi / 5
    return [np.float32(v) for v in (np.cos(a), np.cos(2 * a), np.sin(a), np.sin(2 * a))]


def inverse_envelope(first_pair, offset, table_ref, tile, rows):
    lane = tile * LANES + lax.broadcasted_iota(jnp.int32, (rows, LANES), 1)
    row = lax.broadcasted_iota(jnp.int32, (rows, LANES), 0)
    half = table_ref.shape[1] // 2
    since = 2 * (first_pair + row) + (lane >= half).astype(jnp.int32) - offset
    value = jnp.where(since < 0, 1.0, 1.0)
    for i in range(4):
        value = jnp.where(since >= i, table_ref[i : i + 1, tile * LANES : (tile + 1) * LANES], value)
    return value


def head_kernel(
    scalars,
    x_ref,
    before_ref,
    after_ref,
    cot_ref,
    cot_after_ref,
    conv_w,
    conv_b,
    scale_t,
    shift_t,
    up_w,
    up_b,
    down_w,
    down_b,
    layer_scale,
    head_h,
    head_l,
    head_b,
    ext_w,
    ext_b,
    t1h,
    t1l,
    t2h,
    t2l,
    t0h,
    t0l,
    windows,
    inverse,
    o_norm,
    o_istd,
    o_adt_h,
    o_adt_l,
    o_act_h,
    o_act_l,
    o_slope,
    o_spec,
    o_gm,
    o_gb_h,
    o_gb_l,
    o_gbt_h,
    o_gbt_l,
    o_ghw,
    o_ghb,
    o_ghwe,
    o_ghbe,
    o_gls,
    o_gmb,
    up_h,
    up_l,
    down_h,
    down_l,
    pad4,
    nrm4,
    istd1,
    gs5,
    gm4,
    gl_h,
    gl_l,
    acc_ghb,
    acc_ghwe,
    acc_ghbe,
    acc_gls,
    acc_gmb,
):
    clip, blk = pl.program_id(0), pl.program_id(1)
    clips, blks = pl.num_programs(0), pl.num_programs(1)
    frames, width = x_ref.shape[1], x_ref.shape[2]
    tiles = width // LANES
    start = scalars[0]
    band = scalars[1 + clip]
    local = scalars[1 + clips + clip] - start
    rows8 = before_ref.shape[1]

    @pl.when((clip == 0) & (blk == 0))
    def _():
        up_h[...], up_l[...] = split(up_w[...])
        down_h[...], down_l[...] = split(down_w[...])
        for ref in (o_ghw, acc_ghb, acc_ghwe, acc_ghbe, acc_gls, acc_gmb):
            ref[...] = jnp.zeros_like(ref)

    @pl.when(blk == 0)
    def _():
        def masked(value, first):
            row = first + lax.broadcasted_iota(jnp.int32, value.shape, 0)
            return jnp.where(row >= local, value, 0.0)

        before = masked(before_ref[0], -rows8)
        after = masked(after_ref[0], frames)
        for t in range(tiles):
            lanes = slice(t * LANES, (t + 1) * LANES)
            pad4[t, 0:rows8, :] = before[:, lanes]
            pad4[t, rows8 + frames : 2 * rows8 + frames, :] = after[:, lanes]

        chunk = 64

        def fill(i, carry):
            r = pl.multiple_of(i * chunk, chunk)
            value = masked(x_ref[0, pl.ds(r, chunk), :], r)
            for t in range(tiles):
                pad4[t, pl.ds(r + rows8, chunk), :] = value[:, t * LANES : (t + 1) * LANES]
            return carry

        lax.fori_loop(0, frames // chunk, fill, 0)

        def conv(i, carry):
            r = pl.multiple_of(i * chunk, chunk)
            parts = []
            for t in range(tiles):
                lanes = slice(t * LANES, (t + 1) * LANES)
                total = conv_b[0:1, lanes]
                for k in range(KERNEL):
                    total = total + pad4[t, pl.ds(r + rows8 - 3 + k, chunk), :] * conv_w[k : k + 1, lanes]
                parts.append(total)
            mean = jnp.sum(sum(parts[1:], parts[0]), axis=1, keepdims=True) * (1.0 / width)
            parts = [p - mean for p in parts]
            squares = [p * p for p in parts]
            variance = jnp.sum(sum(squares[1:], squares[0]), axis=1, keepdims=True) * (1.0 / width)
            istd = lax.rsqrt(variance + 1e-6)
            for t in range(tiles):
                nrm4[t, pl.ds(r, chunk), :] = parts[t] * istd
            istd1[pl.ds(r, chunk), :] = jnp.broadcast_to(istd, (chunk, LANES))
            return carry

        lax.fori_loop(0, frames // chunk, conv, 0)

        pairs = frames // 2
        wave_tiles = gs5.shape[0]

        def cotangent(i, carry):
            r = pl.multiple_of(i * chunk, chunk)
            for t in range(wave_tiles):
                first = clips * (wave_tiles * r + t) + clip
                value = cot_ref[pl.ds(first, chunk, stride=clips * wave_tiles), :]
                gs5[t, pl.ds(r, chunk), :] = value * inverse_envelope(r, local, inverse, t, chunk)
            return carry

        lax.fori_loop(0, pairs // chunk, cotangent, 0)
        for t in range(wave_tiles):
            value = cot_after_ref[0, :, t * LANES : (t + 1) * LANES]
            gs5[t, pairs : pairs + 8, :] = value * inverse_envelope(pairs, local, inverse, t, 8)

    base = pl.multiple_of(blk * ROWS, ROWS)
    normed = jnp.concatenate(
        [
            jnp.concatenate([nrm4[t, pl.ds(base + par, PAIRS, stride=2), :] for t in range(tiles)], 1)
            for par in range(2)
        ],
        0,
    )
    o_norm[...] = normed
    for par in range(2):
        o_istd[par * PAIRS : (par + 1) * PAIRS, :] = istd1[pl.ds(base + par, PAIRS, stride=2), :]
    adapted = normed * scale_t[pl.ds(band, 1), :] + shift_t[pl.ds(band, 1), :]
    ad = split(adapted)
    o_adt_h[...], o_adt_l[...] = split(adapted.T)

    hidden = up_h.shape[1]
    step = 256
    for j in range(hidden // step):
        cols = slice(j * step, (j + 1) * step)
        upward = dot3(ad, (up_h[:, cols], up_l[:, cols])) + up_b[0:1, cols]
        cdf = 0.5 + 0.5 * lax.erf(upward * np.float32(0.7071067811865476))
        density = jnp.exp(upward * upward * -0.5) * np.float32(0.3989422804014327)
        o_slope[:, cols] = cdf + upward * density
        o_act_h[:, cols], o_act_l[:, cols] = split(upward * cdf)
    branch = dot3((o_act_h[...], o_act_l[...]), (down_h[...], down_l[...])) + down_b[0:1, :]
    masked_rows = jnp.concatenate(
        [
            jnp.concatenate([pad4[t, pl.ds(base + rows8 + par, PAIRS, stride=2), :] for t in range(tiles)], 1)
            for par in range(2)
        ],
        0,
    )
    residual = masked_rows + layer_scale[0:1, :] * branch
    res = split(residual)
    res_t = split(residual.T)

    first_pair = pl.multiple_of(blk * PAIRS, PAIRS)
    wave_tiles = gs5.shape[0]
    now, one, two = (
        [gs5[t, pl.ds(first_pair + d, PAIRS), :] for t in range(wave_tiles)] for d in range(3)
    )
    mid = wave_tiles // 2
    right = lax.broadcasted_iota(jnp.int32, (PAIRS, LANES), 1) >= LANES // 2
    odd = two[:mid] + [jnp.where(right, now[mid], two[mid])] + now[mid + 1 :] + one
    c1, c2, s1, s2 = fifths()
    folded = []
    for par, segment in enumerate((now + one, odd)):
        seg = [v * windows[par : par + 1, t * LANES : (t + 1) * LANES] for t, v in enumerate(segment)]
        v = [jnp.concatenate(seg[2 * j : 2 * j + 2], 1) for j in range(5)]
        p14, m41, p23, m32 = v[1] + v[4], v[4] - v[1], v[2] + v[3], v[3] - v[2]
        folded.append(
            (
                v[0] + p14 + p23,
                v[0] + c1 * p14 + c2 * p23,
                s1 * m41 + s2 * m32,
                v[0] + c2 * p14 + c1 * p23,
                s2 * m41 - s1 * m32,
            )
        )
    f0, fa, fb, fc, fd = (jnp.concatenate([e, o], 0) for e, o in zip(*folded))
    spectrum_grads = (
        dot3(split(jnp.concatenate([fa, fb], 1)), (t1h[...], t1l[...]), NT),
        dot3(split(jnp.concatenate([fc, fd], 1)), (t2h[...], t2l[...]), NT),
        dot3(split(f0), (t0h[...], t0l[...]), NT),
    )

    ext = split(ext_w[...])
    ext_logits = dot3(ext, res, NT) + ext_b[:, 0:1]
    lane = lax.broadcasted_iota(jnp.int32, (1, ROWS), 1)
    ext_frame = base + jnp.where(lane < PAIRS, 2 * lane, 2 * (lane - PAIRS) + 1)
    ext_present = ext_frame >= local

    def magnitudes(logits, present):
        raw = jnp.where(present, jnp.exp(logits), 0.0)
        squashed = jnp.tanh(raw * np.float32(0.01))
        return 100.0 * squashed, raw * (1.0 - squashed * squashed)

    ext_mag, ext_slope = magnitudes(ext_logits[0:1], ext_present)
    ext_sin, ext_cos = sin_cos(ext_logits[1:2])
    ext_real = ext_mag * ext_cos
    ext_imag = ext_mag * ext_sin
    ext_real_col = jnp.concatenate([ext_real, jnp.zeros((7, ROWS), F32)], 0).T[:, 0:1]

    row = lax.broadcasted_iota(jnp.int32, (PAIRS, 1), 0)
    place = 0
    for index, grads in enumerate(spectrum_grads):
        n = grads.shape[1] // 2
        cols = slice(place, place + 2 * n)
        logits = dot3(res, (head_h[:, cols], head_l[:, cols]))
        for par in range(2):
            rows = slice(par * PAIRS, (par + 1) * PAIRS)
            present = base + 2 * row + par >= local
            value = logits[rows] + head_b[par : par + 1, cols]
            magnitude, slope = magnitudes(value[:, :n], present)
            sine, cosine = sin_cos(value[:, n:])
            real, imag = magnitude * cosine, magnitude * sine
            g_real, g_imag = grads[rows, :n], grads[rows, n:]
            if index == 2:
                corner = lax.broadcasted_iota(jnp.int32, (PAIRS, n), 1) == 0
                shown = jnp.where(corner, ext_real_col[rows], imag)
                g_imag = jnp.where(corner, 0.0, g_imag)
            else:
                shown = imag
            o_spec[rows, place : place + n] = real
            o_spec[rows, place + n : place + 2 * n] = shown
            g_mag = slope * (g_real * cosine + g_imag * sine)
            g_ang = g_imag * real - g_real * imag
            gl = jnp.concatenate([g_mag, g_ang], 1)
            acc_ghb[:, cols] += fold8(gl)
            gl_h[rows, cols], gl_l[rows, cols] = split(gl)
        place += 2 * n

    corner_t = spectrum_grads[2][:, spectrum_grads[2].shape[1] // 2 :].T
    ext_g = corner_t[0:1, :]
    ext_grads = jnp.concatenate(
        [ext_slope * ext_g * ext_cos, -ext_g * ext_imag, jnp.zeros((6, ROWS), F32)], 0
    )
    acc_ghbe[...] += ext_grads
    acc_ghwe[...] += dot3(split(ext_grads), res)
    gl = (gl_h[...], gl_l[...])
    o_ghw[...] += dot3(res_t, gl)
    ext_cols = ext_grads.T
    grad_mixed = (
        dot3(gl, (head_h[...], head_l[...]), NT)
        + ext_cols[:, 0:1] * ext_w[0:1, :]
        + ext_cols[:, 1:2] * ext_w[1:2, :]
    )
    acc_gls[...] += fold8(grad_mixed * branch)
    acc_gmb[...] += fold8(grad_mixed)
    for par in range(2):
        rows = slice(par * PAIRS, (par + 1) * PAIRS)
        for t in range(tiles):
            gm4[t, pl.ds(par, PAIRS, stride=2), :] = grad_mixed[rows, t * LANES : (t + 1) * LANES]
    for t in range(tiles):
        o_gm[:, t * LANES : (t + 1) * LANES] = gm4[t]
    grad_branch = grad_mixed * layer_scale[0:1, :]
    o_gb_h[...], o_gb_l[...] = split(grad_branch)
    o_gbt_h[...], o_gbt_l[...] = split(grad_branch.T)

    @pl.when((clip == clips - 1) & (blk == blks - 1))
    def _():
        o_ghb[...] = jnp.sum(acc_ghb[...], axis=0, keepdims=True)
        o_ghwe[...] = acc_ghwe[...]
        o_ghbe[...] = jnp.sum(acc_ghbe[...], axis=1, keepdims=True)
        o_gls[...] = jnp.sum(acc_gls[...], axis=0, keepdims=True)
        o_gmb[...] = jnp.sum(acc_gmb[...], axis=0, keepdims=True)


def whole(shape):
    return pl.BlockSpec(shape, lambda *_: (0,) * len(shape))


def run_head(scalars, x, before, after, cot, cot_after, weights, head, consts):
    clips, frames, width = x.shape
    blks = frames // ROWS
    count = clips * frames
    hidden = weights[4].shape[1]
    nfft = head[0].shape[1]
    block = lambda i, j, *_: (i * blks + j, 0)
    column = lambda i, j, *_: (0, i * blks + j)
    per_clip = lambda shape: pl.BlockSpec((1,) + shape, lambda i, j, *_: (i, 0, 0))
    in_specs = [per_clip((frames, width)), per_clip(before.shape[1:]), per_clip(after.shape[1:])]
    in_specs += [whole(cot.shape), per_clip(cot_after.shape[1:])]
    operands = list(weights) + list(head) + list(consts)
    in_specs += [whole(v.shape) for v in operands]
    outs = [
        (SDS((count, width), F32), pl.BlockSpec((ROWS, width), block)),
        (SDS((count, LANES), F32), pl.BlockSpec((ROWS, LANES), block)),
        (SDS((width, count), BF16), pl.BlockSpec((width, ROWS), column)),
        (SDS((width, count), BF16), pl.BlockSpec((width, ROWS), column)),
        (SDS((count, hidden), BF16), pl.BlockSpec((ROWS, hidden), block)),
        (SDS((count, hidden), BF16), pl.BlockSpec((ROWS, hidden), block)),
        (SDS((count, hidden), F32), pl.BlockSpec((ROWS, hidden), block)),
        (SDS((count, nfft), F32), pl.BlockSpec((ROWS, nfft), block)),
        (SDS((count, width), F32), pl.BlockSpec((ROWS, width), block)),
        (SDS((count, width), BF16), pl.BlockSpec((ROWS, width), block)),
        (SDS((count, width), BF16), pl.BlockSpec((ROWS, width), block)),
        (SDS((width, count), BF16), pl.BlockSpec((width, ROWS), column)),
        (SDS((width, count), BF16), pl.BlockSpec((width, ROWS), column)),
    ]
    for shape in ((width, nfft), (1, nfft), (8, width), (8, 1), (1, width), (1, width)):
        outs.append((SDS(shape, F32), whole(shape)))
    wave_tiles = nfft // 2 // LANES
    tiles = width // LANES
    scratch = [pltpu.VMEM((width, hidden), BF16)] * 2 + [pltpu.VMEM((hidden, width), BF16)] * 2
    scratch += [
        pltpu.VMEM((tiles, frames + 2 * before.shape[1], LANES), F32),
        pltpu.VMEM((tiles, frames, LANES), F32),
        pltpu.VMEM((frames, LANES), F32),
        pltpu.VMEM((wave_tiles, frames // 2 + 8, LANES), F32),
        pltpu.VMEM((tiles, ROWS, LANES), F32),
        pltpu.VMEM((ROWS, nfft), BF16),
        pltpu.VMEM((ROWS, nfft), BF16),
        pltpu.VMEM((8, nfft), F32),
        pltpu.VMEM((8, width), F32),
        pltpu.VMEM((8, ROWS), F32),
        pltpu.VMEM((8, width), F32),
        pltpu.VMEM((8, width), F32),
    ]
    return pl.pallas_call(
        head_kernel,
        grid_spec=pltpu.PrefetchScalarGridSpec(
            num_scalar_prefetch=1,
            grid=(clips, blks),
            in_specs=in_specs,
            out_specs=[s for _, s in outs],
            scratch_shapes=scratch,
        ),
        out_shape=[s for s, _ in outs],
        compiler_params=pltpu.CompilerParams(vmem_limit_bytes=VMEM),
        name="head",
    )(scalars, x, before, after, cot, cot_after, *operands)


def ffn_kernel(
    gb_h, gb_l, gbt_h, gbt_l, act_h, act_l, slope, adt_h, adt_l, down_w,
    o_gdn, o_gup, o_gub, o_gu_h, o_gu_l, dw_h, dw_l, acc_gub,
):
    step = pl.program_id(0)

    @pl.when(step == 0)
    def _():
        dw_h[...], dw_l[...] = split(down_w[...])
        for ref in (o_gdn, o_gup, acc_gub):
            ref[...] = jnp.zeros_like(ref)

    o_gdn[...] += dot3((gbt_h[...], gbt_l[...]), (act_h[...], act_l[...]))
    cols = 256
    for j in range(slope.shape[1] // cols):
        part = slice(j * cols, (j + 1) * cols)
        gu = dot3((gb_h[...], gb_l[...]), (dw_h[part, :], dw_l[part, :]), NT) * slope[:, part]
        acc_gub[:, part] += fold8(gu)
        gs = split(gu)
        o_gu_h[:, part], o_gu_l[:, part] = gs
        o_gup[:, part] += dot3((adt_h[...], adt_l[...]), gs)

    @pl.when(step == pl.num_programs(0) - 1)
    def _():
        o_gub[...] = jnp.sum(acc_gub[...], axis=0, keepdims=True)


def run_ffn(gb, gbt, act, slope, adt, down_w, part, parts):
    count, width = gb[0].shape
    hidden = slope.shape[1] // parts
    rows = 512
    row = lambda i: (i, 0)
    mine = lambda i: (i, part)
    col = lambda i: (0, i)
    in_specs = [pl.BlockSpec((rows, width), row)] * 2 + [pl.BlockSpec((width, rows), col)] * 2
    in_specs += [pl.BlockSpec((rows, hidden), mine)] * 3 + [pl.BlockSpec((width, rows), col)] * 2
    in_specs += [pl.BlockSpec((hidden, width), lambda i: (part, 0))]
    return pl.pallas_call(
        ffn_kernel,
        grid=(count // rows,),
        in_specs=in_specs,
        out_specs=[
            whole((width, hidden)),
            whole((width, hidden)),
            whole((1, hidden)),
            pl.BlockSpec((rows, hidden), row),
            pl.BlockSpec((rows, hidden), row),
        ],
        out_shape=[
            SDS((width, hidden), F32),
            SDS((width, hidden), F32),
            SDS((1, hidden), F32),
            SDS((count, hidden), BF16),
            SDS((count, hidden), BF16),
        ],
        scratch_shapes=[pltpu.VMEM((hidden, width), BF16)] * 2 + [pltpu.VMEM((8, hidden), F32)],
        compiler_params=pltpu.CompilerParams(vmem_limit_bytes=VMEM),
        name="ffn_grads",
    )(*gb, *gbt, *act, slope, *adt, down_w)


def norm_kernel(parts, scalars, *refs):
    gu = refs[: 2 * parts]
    up_w, norm, istd, scale_t, o_gh, o_scale, o_shift, up_h, up_l, nat4, acc_scale, acc_shift = refs[2 * parts :]
    clip, blk = pl.program_id(0), pl.program_id(1)
    clips, blks = pl.num_programs(0), pl.num_programs(1)
    band = scalars[1 + clip]
    width = norm.shape[1]
    tiles = width // LANES

    @pl.when((clip == 0) & (blk == 0))
    def _():
        up_h[...], up_l[...] = split(up_w[...])
        o_scale[...] = jnp.zeros_like(o_scale)
        o_shift[...] = jnp.zeros_like(o_shift)

    @pl.when(blk == 0)
    def _():
        acc_scale[...] = jnp.zeros_like(acc_scale)
        acc_shift[...] = jnp.zeros_like(acc_shift)

    hidden = up_w.shape[1] // parts
    ga = None
    for j in range(parts):
        cols = slice(j * hidden, (j + 1) * hidden)
        term = dot3((gu[2 * j][...], gu[2 * j + 1][...]), (up_h[:, cols], up_l[:, cols]), NT)
        ga = term if ga is None else ga + term
    normed = norm[...]
    acc_scale[...] += fold8(ga * normed)
    acc_shift[...] += fold8(ga)
    gn = ga * scale_t[pl.ds(band, 1), :]
    mean = jnp.sum(gn, axis=1, keepdims=True) * (1.0 / width)
    along = jnp.sum(gn * normed, axis=1, keepdims=True) * (1.0 / width)
    gh = istd[:, 0:1] * (gn - mean - normed * along)
    half = norm.shape[0] // 2
    for par in range(2):
        for t in range(tiles):
            nat4[t, pl.ds(par, half, stride=2), :] = gh[par * half : (par + 1) * half, t * LANES : (t + 1) * LANES]
    for t in range(tiles):
        o_gh[:, t * LANES : (t + 1) * LANES] = nat4[t]

    @pl.when(blk == blks - 1)
    def _():
        o_scale[pl.ds(band, 1), :] += jnp.sum(acc_scale[...], axis=0, keepdims=True)
        o_shift[pl.ds(band, 1), :] += jnp.sum(acc_shift[...], axis=0, keepdims=True)


def run_norm(scalars, gus, up_w, norm, istd, scale_t, clips):
    count, width = norm.shape
    blks = count // clips // ROWS
    parts = len(gus)
    block = lambda i, j, *_: (i * blks + j, 0)
    flat = [v for pair in gus for v in pair]
    in_specs = [pl.BlockSpec((ROWS, v.shape[1]), block) for v in flat]
    in_specs += [whole(up_w.shape), pl.BlockSpec((ROWS, width), block)]
    in_specs += [pl.BlockSpec((ROWS, LANES), block), whole(scale_t.shape)]
    return pl.pallas_call(
        functools.partial(norm_kernel, parts),
        grid_spec=pltpu.PrefetchScalarGridSpec(
            num_scalar_prefetch=1,
            grid=(clips, blks),
            in_specs=in_specs,
            out_specs=[pl.BlockSpec((ROWS, width), block), whole(scale_t.shape), whole(scale_t.shape)],
            scratch_shapes=[pltpu.VMEM(up_w.shape, BF16)] * 2
            + [pltpu.VMEM((width // LANES, ROWS, LANES), F32)]
            + [pltpu.VMEM((8, width), F32)] * 2,
        ),
        out_shape=[SDS((count, width), F32), SDS(scale_t.shape, F32), SDS(scale_t.shape, F32)],
        compiler_params=pltpu.CompilerParams(vmem_limit_bytes=VMEM),
        name="norm_grads",
    )(scalars, *flat, up_w, norm, istd, scale_t)


def conv_kernel(
    scalars, x_ref, before_ref, after_ref, gh_ref, gh_before, gh_after, gm_ref, conv_w,
    o_gi, o_gcw, o_gcb, pad4, gh4, acc_w, acc_b,
):
    clip = pl.program_id(0)
    clips = pl.num_programs(0)
    frames, width = x_ref.shape[1], x_ref.shape[2]
    tiles = width // LANES
    local = scalars[1 + clips + clip] - scalars[0]
    rows8 = before_ref.shape[1]
    chunk = 64

    @pl.when(clip == 0)
    def _():
        acc_w[...] = jnp.zeros_like(acc_w)
        acc_b[...] = jnp.zeros_like(acc_b)

    def masked(value, first):
        row = first + lax.broadcasted_iota(jnp.int32, value.shape, 0)
        return jnp.where(row >= local, value, 0.0)

    before, after = masked(before_ref[0], -rows8), masked(after_ref[0], frames)
    for t in range(tiles):
        lanes = slice(t * LANES, (t + 1) * LANES)
        pad4[t, 0:rows8, :] = before[:, lanes]
        pad4[t, rows8 + frames : 2 * rows8 + frames, :] = after[:, lanes]
        gh4[t, 0:rows8, :] = gh_before[0, :, lanes]
        gh4[t, rows8 + frames : 2 * rows8 + frames, :] = gh_after[0, :, lanes]

    def fill(i, carry):
        r = pl.multiple_of(i * chunk, chunk)
        value = masked(x_ref[0, pl.ds(r, chunk), :], r)
        for t in range(tiles):
            lanes = slice(t * LANES, (t + 1) * LANES)
            pad4[t, pl.ds(r + rows8, chunk), :] = value[:, lanes]
            gh4[t, pl.ds(r + rows8, chunk), :] = gh_ref[0, pl.ds(r, chunk), lanes]
        return carry

    lax.fori_loop(0, frames // chunk, fill, 0)

    def conv(i, carry):
        r = pl.multiple_of(i * chunk, chunk)
        shown = r + lax.broadcasted_iota(jnp.int32, (chunk, LANES), 0) >= local
        for t in range(tiles):
            lanes = slice(t * LANES, (t + 1) * LANES)
            gh = gh4[t, pl.ds(r + rows8, chunk), :]
            acc_b[:, lanes] += fold8(gh)
            total = gm_ref[0, pl.ds(r, chunk), lanes]
            for k in range(KERNEL):
                total = total + conv_w[k : k + 1, lanes] * gh4[t, pl.ds(r + rows8 + 3 - k, chunk), :]
                acc_w[8 * k : 8 * k + 8, lanes] += fold8(gh * pad4[t, pl.ds(r + rows8 - 3 + k, chunk), :])
            o_gi[0, pl.ds(r, chunk), lanes] = jnp.where(shown, total, 0.0)
        return carry

    lax.fori_loop(0, frames // chunk, conv, 0)

    @pl.when(clip == clips - 1)
    def _():
        for k in range(KERNEL):
            o_gcw[k : k + 1, :] = jnp.sum(acc_w[8 * k : 8 * k + 8, :], axis=0, keepdims=True)
        o_gcb[...] = jnp.sum(acc_b[...], axis=0, keepdims=True)


def run_conv(scalars, x, before, after, gh, gh_before, gh_after, gm, conv_w):
    clips, frames, width = x.shape
    rows8 = before.shape[1]
    per_clip = lambda n: pl.BlockSpec((1, n, width), lambda i, *_: (i, 0, 0))
    padded = pltpu.VMEM((width // LANES, frames + 2 * rows8, LANES), F32)
    return pl.pallas_call(
        conv_kernel,
        grid_spec=pltpu.PrefetchScalarGridSpec(
            num_scalar_prefetch=1,
            grid=(clips,),
            in_specs=[per_clip(n) for n in (frames, rows8, rows8, frames, rows8, rows8, frames)]
            + [whole(conv_w.shape)],
            out_specs=[per_clip(frames), whole(conv_w.shape), whole((1, width))],
            scratch_shapes=[padded, padded, pltpu.VMEM((8 * KERNEL, width), F32), pltpu.VMEM((8, width), F32)],
        ),
        out_shape=[SDS(x.shape, F32), SDS(conv_w.shape, F32), SDS((1, width), F32)],
        compiler_params=pltpu.CompilerParams(vmem_limit_bytes=VMEM),
        name="conv_grads",
    )(scalars, x, before, after, gh, gh_before, gh_after, gm, conv_w)


def wave_kernel(
    scalars, spec, t1h, t1l, t2h, t2l, t0h, t0l, windows, inverse, o_wave, o_tail, acc5
):
    clip, blk = pl.program_id(0), pl.program_id(1)
    clips, blks = pl.num_programs(0), pl.num_programs(1)
    local = scalars[1 + clips + clip] - scalars[0]
    tiles = acc5.shape[0]

    @pl.when(blk == 0)
    def _():
        acc5[...] = jnp.zeros_like(acc5)

    @pl.when(blk > 0)
    def _():
        for t in range(tiles):
            acc5[t, 0:8, :] = acc5[t, PAIRS : PAIRS + 8, :]
            acc5[t, 8:, :] = jnp.zeros((PAIRS, LANES), F32)

    n1, n2 = t1h.shape[0], t2h.shape[0]
    ab = dot3(split(spec[:, :n1]), (t1h[...], t1l[...]))
    cd = dot3(split(spec[:, n1 : n1 + n2]), (t2h[...], t2l[...]))
    p0 = dot3(split(spec[:, n1 + n2 :]), (t0h[...], t0l[...]))
    c1, c2, s1, s2 = fifths()
    sides = []
    for par in range(2):
        rows = slice(par * PAIRS, (par + 1) * PAIRS)
        w = p0.shape[1]
        a, b, c, d, p = ab[rows, :w], ab[rows, w:], cd[rows, :w], cd[rows, w:], p0[rows]
        e1, o1 = p + c1 * a + c2 * c, s1 * b + s2 * d
        e2, o2 = p + c2 * a + c1 * c, s2 * b - s1 * d
        v = [p + a + c, e1 - o1, e2 - o2, e2 + o2, e1 + o1]
        seg = []
        for t in range(2 * tiles):
            part = v[t // 2][:, (t % 2) * LANES : (t % 2 + 1) * LANES]
            seg.append(part * windows[par : par + 1, t * LANES : (t + 1) * LANES])
        sides.append(seg)
    even, odd = sides
    mid = tiles // 2
    right = lax.broadcasted_iota(jnp.int32, (PAIRS, LANES), 1) >= LANES // 2
    for t in range(tiles):
        here = even[t]
        if t > mid:
            here = here + odd[t]
        if t == mid:
            here = here + jnp.where(right, odd[t], 0.0)
        acc5[t, 0:PAIRS, :] += here
        acc5[t, 1 : PAIRS + 1, :] += even[tiles + t] + odd[tiles + t]
        if t < mid:
            acc5[t, 2 : PAIRS + 2, :] += odd[t]
        if t == mid:
            acc5[t, 2 : PAIRS + 2, :] += jnp.where(right, 0.0, odd[t])
        first = pl.multiple_of(blk * PAIRS, PAIRS)
        value = acc5[t, 0:PAIRS, :] * inverse_envelope(first, local, inverse, t, PAIRS)
        o_wave[pl.ds(clips * (tiles * first + t) + clip, PAIRS, stride=clips * tiles), :] = value

    @pl.when(blk == blks - 1)
    def _():
        for t in range(tiles):
            o_tail[0, :, t * LANES : (t + 1) * LANES] = acc5[t, PAIRS : PAIRS + 8, :]


def run_wave(scalars, spec, consts, clips):
    count, nfft = spec.shape
    blks = count // clips // ROWS
    tiles = nfft // 2 // LANES
    chunks = count * nfft // 4 // LANES
    return pl.pallas_call(
        wave_kernel,
        grid_spec=pltpu.PrefetchScalarGridSpec(
            num_scalar_prefetch=1,
            grid=(clips, blks),
            in_specs=[pl.BlockSpec((ROWS, nfft), lambda i, j, *_: (i * blks + j, 0))]
            + [whole(v.shape) for v in consts],
            out_specs=[
                whole((chunks, LANES)),
                pl.BlockSpec((1, 8, nfft // 2), lambda i, j, *_: (i, 0, 0)),
            ],
            scratch_shapes=[pltpu.VMEM((tiles, PAIRS + 8, LANES), F32)],
        ),
        out_shape=[SDS((chunks, LANES), F32), SDS((clips, 8, nfft // 2), F32)],
        compiler_params=pltpu.CompilerParams(vmem_limit_bytes=VMEM),
        name="wave",
    )(scalars, spec, *consts)


def neighbours(last, first, axis):
    devices = lax.axis_size(axis)
    up = [(i, i + 1) for i in range(devices - 1)]
    down = [(j, i) for i, j in up]
    return lax.ppermute(last, axis, up), lax.ppermute(first, axis, down)


def to_chunks(wave):
    clips, samples = wave.shape
    return wave.reshape(clips, samples // LANES, LANES).transpose(1, 0, 2).reshape(-1, LANES)


def from_chunks(chunks, clips):
    rows = chunks.shape[0] // clips
    return chunks.reshape(rows, clips, LANES).transpose(1, 0, 2).reshape(clips, rows * LANES)


def body(
    inputs,
    band_ids,
    offsets,
    conv_weight,
    conv_bias,
    scale_table,
    shift_table,
    up_weight,
    up_bias,
    down_weight,
    down_bias,
    layer_scale,
    head_weight,
    head_bias,
    wave_cotangent,
):
    clips, frames, width = inputs.shape
    nfft = head_weight.shape[1] - 2
    half = nfft // 2
    start = lax.axis_index("tm") * frames
    scalars = jnp.concatenate([start[None].astype(jnp.int32), band_ids, offsets])
    transforms, windows, inverse, order, turns, _ = tables(nfft)
    dft = [jnp.asarray(v) for pair in transforms for v in pair]
    consts = dft + [jnp.asarray(windows), jnp.asarray(inverse)]

    before, after = neighbours(inputs[:, -8:], inputs[:, :8], "tm")
    _, cot_after = neighbours(wave_cotangent[:, : 2 * half], wave_cotangent[:, : 2 * half], "tm")
    cot_after = jnp.pad(cot_after.reshape(clips, 2, half), ((0, 0), (0, 6), (0, 0)))

    place = np.zeros((nfft + 2, nfft), np.float32)
    place[order, np.arange(nfft)] = 1.0
    place = jnp.asarray(place.astype(ml_dtypes.bfloat16))
    head_high = lax.reduce_precision(head_weight, 8, 7)
    head_h = dot(head_high.astype(BF16), place).astype(BF16)
    head_l = dot((head_weight - head_high).astype(BF16), place).astype(BF16)
    bias = jnp.dot(head_bias[None], place.astype(F32), precision=lax.Precision.HIGHEST)
    bias = jnp.concatenate([bias, bias + turns[None]], 0)
    ends = jnp.asarray([half, nfft + 1])
    ext_w = jnp.concatenate([head_weight[:, half : half + 1], head_weight[:, nfft + 1 :]], 1).T
    ext_w = jnp.pad(ext_w, ((0, 6), (0, 0)))
    ext_b = jnp.pad(jnp.stack([head_bias[half], head_bias[nfft + 1]])[:, None], ((0, 6), (0, 0)))

    weights = (
        conv_weight,
        conv_bias[None],
        scale_table,
        shift_table,
        up_weight,
        up_bias[None],
        down_weight,
        down_bias[None],
        layer_scale[None],
    )
    (
        norm, istd, adt_h, adt_l, act_h, act_l, slope, spec, gm, gb_h, gb_l, gbt_h, gbt_l,
        ghw, ghb, ghwe, ghbe, gls, gmb,
    ) = run_head(
        scalars, inputs, before, after, to_chunks(wave_cotangent), cot_after, weights,
        (head_h, head_l, bias, ext_w, ext_b), consts,
    )

    parts = 3
    gdn, gup, gub, gus = [], [], [], []
    for part in range(parts):
        down, up, up_b, gu_h, gu_l = run_ffn(
            (gb_h, gb_l), (gbt_h, gbt_l), (act_h, act_l), slope, (adt_h, adt_l), down_weight, part, parts
        )
        gdn.append(down)
        gup.append(up)
        gub.append(up_b)
        gus.append((gu_h, gu_l))
    gh, gscale, gshift = run_norm(scalars, gus, up_weight, norm, istd, scale_table, clips)
    gh = gh.reshape(clips, frames, width)
    gh_before, gh_after = neighbours(gh[:, -8:], gh[:, :8], "tm")
    gm = gm.reshape(clips, frames, width)
    grad_inputs, gcw, gcb = run_conv(scalars, inputs, before, after, gh, gh_before, gh_after, gm, conv_weight)

    wave, tail = run_wave(scalars, spec, consts, clips)
    arrived, _ = neighbours(tail[:, :2].reshape(clips, nfft), tail[:, :2].reshape(clips, nfft), "tm")
    arrived = arrived * jnp.tile(jnp.asarray(inverse[3:4]), (1, 2))
    head_rows = clips * nfft // LANES
    wave = wave.at[:head_rows].add(to_chunks(arrived))
    waveform = from_chunks(wave, clips)

    sums = lax.psum(
        (gcw, gcb, gscale, gshift, *gup, *gub, *gdn, gmb, gls, ghw, ghwe, ghb, ghbe), ("clip", "tm")
    )
    gcw, gcb, gscale, gshift = sums[:4]
    gup, gub, gdn = sums[4 : 4 + parts], sums[4 + parts : 4 + 2 * parts], sums[4 + 2 * parts : 4 + 3 * parts]
    gmb, gls, ghw, ghwe, ghb, ghbe = sums[4 + 3 * parts :]
    ghw_high = lax.reduce_precision(ghw, 8, 7)
    ghw = dot(ghw_high.astype(BF16), place, NT) + dot((ghw - ghw_high).astype(BF16), place, NT)
    ghw = ghw.at[:, half].set(ghwe[0]).at[:, nfft + 1].set(ghwe[1])
    ghb = jnp.dot(ghb, place.astype(F32).T, precision=lax.Precision.HIGHEST)[0]
    ghb = ghb.at[half].set(ghbe[0, 0]).at[nfft + 1].set(ghbe[1, 0])
    return (
        waveform,
        grad_inputs,
        gcw,
        gcb[0],
        gscale,
        gshift,
        jnp.concatenate(gup, 1),
        jnp.concatenate(gub, 1)[0],
        jnp.concatenate([g.T for g in gdn], 0),
        gmb[0] * layer_scale,
        gls[0],
        ghw,
        ghb,
    )


def solution(mesh):
    in_specs = (P("clip", "tm", None), P("clip"), P("clip")) + (P(),) * 11 + (P("clip", "tm"),)
    out_specs = (P("clip", "tm"), P("clip", "tm", None)) + (P(),) * 11
    return jax.shard_map(body, mesh=mesh, in_specs=in_specs, out_specs=out_specs, check_vma=False)
```

time: 726 us -> 403 us (0.56)
  matrix products: 347 us -> 19.6 us
  Pallas kernels: 0 us -> 196 us
  other arithmetic: 125 us -> 13.4 us
  local copies, waits for them, and re-layouts: 98.8 us -> 18.4 us
  waiting for transfers between devices: 72.6 us -> 83.9 us
    dot_general x15 -> x6, matrix products: 347 us -> 19.6 us  [the longest x4 15.5 us: dot(): return lax.dot_general(a, b, dims, preferred_element_type=F32)]
    pallas_call x0 -> x7, Pallas kernels: none -> 196 us  [the longest x1 90.4 us: run_head(): pl.pallas_call(head_kernel, grid_spec=pltpu.PrefetchScalarGridSpec(num_sc...]
    mul x5 -> x2, other arithmetic: 60.3 us -> 0.59 us  [the longest x1 0.58 us: body(): gmb[0] * layer_scale]
    reshape x12 -> x2, local copies, waits for them, and re-layouts: 39.7 us -> 0.03 us  [the longest x1 0.02 us: body(): cot_after.reshape(clips, 2, half)]
    reduce_sum x5 -> x0, other arithmetic: 36.3 us -> none  [the longest x1 19.7 us: body(): jnp.sum(padded[:, kernel_pos:kernel_pos + frames] * grad_conved, axis=(0,...]
    unnamed x179 -> x54, local copies, waits for them, and re-layouts: 35.5 us -> 7.15 us
    div x6 -> x0, other arithmetic: 11.4 us -> none  [the longest x2 7.06 us: body(): wave_cotangent.reshape(clip_count, frames, hop_size) / envelope]
    another operation x2, local copies, waits for them, and re-layouts: 10.4 us -> 0.02 us  [the longest x1 10.4 us: body(): jnp.stack([grad_extended[:, quarter:quarter + frames] for quarter in rang...]
  transfers between devices with their start and end apart: 7 -> 7, of which waited for: 1 -> 2; matrix products, arithmetic and copies ran while one was open for 26% -> 7% of each run, Pallas kernels for 0% -> 12%
where the time goes in v1:
time: 403 us; the launch traced here: 402 us
  Pallas kernels  196 us (49%)
  waiting for transfers between devices  83.9 us (21%)
  blocking collectives  42.1 us (10%)
  matrix products  19.6 us (5%)
  local copies, waits for them, and re-layouts  18.4 us (5%)
  starting transfers between devices  14.5 us (4%)
  between operations  14.5 us (4%)
  other arithmetic  13.4 us (3%)
    pallas_call x1, Pallas kernels, run_head(): pl.pallas_call(head_kernel, grid_spec=pltpu.PrefetchScalarGridSpec(num_sc...  90.4 us
    psum x1, waiting for transfers between devices, body(): lax.psum((gcw, gcb, gscale, gshift, *gup, *gub, *gdn, gmb, gls, ghw, ghwe...  81.6 us
    pallas_call x3, Pallas kernels, run_ffn(): pl.pallas_call(ffn_kernel, grid=(count // rows,), in_specs=in_specs, out_...  58.9 us
    psum x1, blocking collectives, body(): lax.psum((gcw, gcb, gscale, gshift, *gup, *gub, *gdn, gmb, gls, ghw, ghwe...  42.1 us
    pallas_call x1, Pallas kernels, run_norm(): pl.pallas_call(functools.partial(norm_kernel, parts), grid_spec=pltpu.Pre...  18.4 us
    pallas_call x1, Pallas kernels, run_wave(): pl.pallas_call(wave_kernel, grid_spec=pltpu.PrefetchScalarGridSpec(num_sc...  16.8 us
    dot_general x4, matrix products, dot(): return lax.dot_general(a, b, dims, preferred_element_type=F32)  15.5 us
    ppermute x6, starting transfers between devices, neighbours(): return (lax.ppermute(last, axis, up), lax.ppermute(first, axis, down))  14.5 us
  transfers between devices with their start and end apart: 7, of which 2 were waited for; matrix products, arithmetic and copies ran while one was open for 7% of the time, Pallas kernels for 12%

profile of v1, /device:TPU:0, one launch (start us, length us, event | category | flops | bytes accessed | tf_op | source)
XLA Modules:
  0.0 402.2 jit_solution(14823600911826388358)
XLA Ops:
  7.2 0.8 fusion.7
  8.0 4.9 %collective-permute-start = (f32[2,8,512]{2,1,0:T(8,128)S(1)}, f32[2,8,512]{2,1,0:T(8,128)S(1)}, u32[]{:S(2)}, u32[]{:S(2)}) collective-permute-start(f32[2,8,512]{2,1,0:T(8,128)S(1)} %get-tuple-element.205), channel_id=1, source_target_pairs={{0,1},{2,3},{4,5},{6,7},{8,9},{10,11},{12,13},{14,15},{16,17},{18,... | collective-permute-start | bytes 98312 | tf_op jit(solution)/shard_map/ppermute | solution.py:781
  12.9 1.3 collective-permute-start.1
  14.2 0.7 slice.115
  14.9 1.3 collective-permute-start.2
  16.2 6.2 %fusion.head_h = bf16[512,1280]{1,0:T(8,128)(2,1)} fusion(bf16[1282,1280]{1,0:T(8,128)(2,1)} %constant.165.clone, f32[512,1282]{0,1:T(8,128)} %param.48), kind=kOutput, calls=%fused_computation.9 | convolution fusion | flops 1682311168 | bytes 7218176 | tf_op jit(solution)/shard_map/dot_general | solution.py:34
  22.4 3.5 convolution_convert_fusion.head_l
  25.9 0.6 fusion.9
  26.5 1.4 fusion.11
  27.9 0.6 pad_maximum_fusion.2.head_b
  28.5 1.4 maximum_bitcast_fusion.1
  30.5 0.6 broadcast_in_dim.21.up_b
  31.2 0.6 pad.23.ext_w
  31.8 0.6 pad.24.ext_b
  32.4 0.6 pad.22.cot_after_ref
  33.1 0.6 copy-done.1
  33.7 90.4 %head.1 = (f32[2048,512]{1,0:T(8,128)}, f32[2048,128]{1,0:T(8,128)}, bf16[512,2048]{1,0:T(8,128)(2,1)}, bf16[512,2048]{1,0:T(8,128)(2,1)}, bf16[2048,1536]{1,0:T...) custom-call(s32[5]{0:T(128)} %pad_add_fusion.scalars, ...), custom_call_target="tpu_custom_call" | custom-call | tf_op jit(solution)/shard_map/head/pallas_call | solution.py:460
  124.1 19.6 %ffn_grads.3 = (f32[512,512]{1,0:T(8,128)}, f32[512,512]{1,0:T(8,128)}, f32[1,512]{1,0:T(1,128)}, bf16[2048,512]{1,0:T(8,128)(2,1)}, bf16[2048,512]{1,0:T(8,128)(2,1)}) custom-call(bf16[2048,512]{1,0:T(8,128)(2,1)} %get-tuple-element.118.gb_h, bf16[2048,512]{1,0:T(8,128)(2,1)} %get-tuple-element.119.gb_l, bf16[512,2048]{1,0:T(8,128)(2,1)} %get-tuple-element.120.gbt_h, ...), custom_call_target="tpu_custom_call" | custom-call | tf_op jit(solution)/shard_map/ffn_grads/pallas_call | solution.py:512
  143.7 19.8 %ffn_grads.4 = (f32[512,512]{1,0:T(8,128)}, f32[512,512]{1,0:T(8,128)}, f32[1,512]{1,0:T(1,128)}, bf16[2048,512]{1,0:T(8,128)(2,1)}, bf16[2048,512]{1,0:T(8,128)(2,1)}) custom-call(bf16[2048,512]{1,0:T(8,128)(2,1)} %get-tuple-element.118.gb_h, bf16[2048,512]{1,0:T(8,128)(2,1)} %get-tuple-element.119.gb_l, bf16[512,2048]{1,0:T(8,128)(2,1)} %get-tuple-element.120.gbt_h, ...), custom_call_target="tpu_custom_call" | custom-call | tf_op jit(solution)/shard_map/ffn_grads/pallas_call | solution.py:512
  163.5 19.5 %ffn_grads.5 = (f32[512,512]{1,0:T(8,128)}, f32[512,512]{1,0:T(8,128)}, f32[1,512]{1,0:T(1,128)}, bf16[2048,512]{1,0:T(8,128)(2,1)}, bf16[2048,512]{1,0:T(8,128)(2,1)}) custom-call(bf16[2048,512]{1,0:T(8,128)(2,1)} %get-tuple-element.118.gb_h, bf16[2048,512]{1,0:T(8,128)(2,1)} %get-tuple-element.119.gb_l, bf16[512,2048]{1,0:T(8,128)(2,1)} %get-tuple-element.120.gbt_h, ...), custom_call_target="tpu_custom_call" | custom-call | tf_op jit(solution)/shard_map/ffn_grads/pallas_call | solution.py:512
  183.0 0.7 compare_reduce_fusion
  183.7 16.8 %wave.1 = (f32[5120,128]{1,0:T(8,128)}, f32[2,8,640]{2,1,0:T(8,128)}) custom-call(s32[5]{0:T(128)} %pad_add_fusion.scalars, f32[2048,1280]{1,0:T(8,128)} %get-tuple-element.115.spec, bf16[512,512]{1,0:T(8,128)(2,1)} %constant.157.clone.t1h, bf16[512,512]{1,0:T(8,128)(2,1)} %constant.158.clone.t1l, bf16[512,512]{1,0:T(8,128)(2,1)} %constant.159.clone.t2h, ...), custom_call_target="tpu_custom_call" | custom-call | tf_op jit(solution)/shard_map/wave/pallas_call | solution.py:758
  200.6 0.8 slice_bitcast_fusion
  201.3 4.5 %collective-permute-start.3 = (f32[2,1280]{1,0:T(2,128)S(1)}, f32[2,1280]{1,0:T(2,128)S(1)}, u32[]{:S(2)}, u32[]{:S(2)}) collective-permute-start(f32[2,1280]{1,0:T(2,128)S(1)} %bitcast.58), channel_id=1, source_target_pairs={{0,1},{2,3},{4,5},{6,7},{8,9},{10,11},{12,13},{14,15},{16,17},{18,... | collective-permute-start | bytes 30728 | tf_op jit(solution)/shard_map/ppermute | solution.py:781
  205.9 18.4 %norm_grads.1 = (f32[2048,512]{1,0:T(8,128)}, f32[4,512]{1,0:T(4,128)}, f32[4,512]{1,0:T(4,128)}) custom-call(s32[5]{0:T(128)} %pad_add_fusion.scalars, bf16[2048,512]{1,0:T(8,128)(2,1)} %get-tuple-element.127.refs_0_, bf16[2048,512]{1,0:T(8,128)(2,1)} %get-tuple-element.128.refs_1_, bf16[2048,512]{1,0:T(8,128)(2,1)} %get-tuple-element.129.refs_2_, ...), custom_call_target="tpu_custom_call" | custom-call | tf_op jit(solution)/shard_map/norm_grads/pallas_call | solution.py:591
  224.3 0.8 fusion.6
  225.1 1.3 collective-permute-start.4
  226.4 1.3 collective-permute-start.5
  227.8 0.7 slice_add_fusion
  228.5 1.3 scatter-add.4
  229.8 2.3 collective-permute-done.5.gh_after
  232.2 0.6 copy-done.4
  232.9 11.2 %conv_grads.1 = (f32[2,1024,512]{2,1,0:T(8,128)}, f32[7,512]{1,0:T(8,128)}, f32[1,512]{1,0:T(1,128)}) custom-call(s32[5]{0:T(128)} %pad_add_fusion.scalars, f32[2,1024,512]{2,1,0:T(8,128)} %x_ref.3, f32[2,8,512]{2,1,0:T(8,128)} %copy-done.1, f32[2,8,512]{2,1,0:T(8,128)} %copy-done.2, f32[2,1024,512]{2,1,0:T(8,128)} %bitcast.51, f32[2,8,512]{2,1,0:T(8,128)} %copy-done.3, ...), custom_call_target="tpu_custom_call" | custom-call | tf_op jit(solution)/shard_map/conv_grads/pallas_call | solution.py:676
  244.1 42.1 %all-reduce.3 = (f32[7,512]{1,0:T(8,128)}, f32[512]{0:T(512)}, f32[4,512]{1,0:T(4,128)}, f32[4,512]{1,0:T(4,128)}, f32[1,512]{1,0:T(1,128)S(1)}, /*index=5*/f32[...) all-reduce(f32[7,512]{1,0:T(8,128)} %get-tuple-element.138, ...), channel_id=1, replica_groups=mesh['clip'=16,'tm'=2] {'clip','tm'}, use_global_device_ids=true, to_apply=%region_0.1 | all-reduce | flops 16136 | bytes 129088 | tf_op jit(solution)/shard_map/psum | solution.py:879
  287.3 2.7 convolution_reduce_fusion
  290.0 0.7 bitcast_dynamic-update-slice_fusion.1
  290.7 0.7 bitcast_dynamic-update-slice_fusion
  291.4 0.6 maximum_reduce_fusion
  292.0 81.6 %all-reduce.7.cloned.1.call-done = (f32[512,512]{1,0:T(8,128)}, f32[512,512]{1,0:T(8,128)}, f32[512,512]{1,0:T(8,128)}, f32[512,512]{0,1:T(8,128)}, f32[512,512]...) async-done(((f32[512,512]{1,0:T(8,128)}, f32[512,512]{1,0:T(8,128)}, f32[512,512]{1,0:T(8,128)}, f32[512,512]{0,1:T(8,128)}, f32[512,512]{0,1:T(8,128)}, ...) | async-done | bytes 8912912 | tf_op jit(solution)/shard_map/psum | solution.py:879
  373.5 3.8 pad_maximum_fusion.1
  377.3 3.5 copy.50
  380.8 3.8 fusion.4
  384.7 2.0 convolution_add_fusion
  386.7 1.5 copy-done.23
  388.2 0.7 broadcast_select_fusion
  388.9 1.3 scatter.14
  390.3 3.8 pad_maximum_fusion
  394.0 1.3 scatter.15
  (70 shorter events, 2.1 us)
Async XLA Ops:
  7.2 366.4 %all-reduce.7.cloned.1.call-start = ((), (), s32[]{:S(2)}) async-start(), calls=%async_computation | async-start | bytes 17825792 | tf_op jit(solution)/shard_map/psum | solution.py:879
  8.0 25.0 %collective-permute-start = (f32[2,8,512]{2,1,0:T(8,128)S(1)}, f32[2,8,512]{2,1,0:T(8,128)S(1)}, u32[]{:S(2)}, u32[]{:S(2)}) collective-permute-start(f32[2,8,512]{2,1,0:T(8,128)S(1)} %get-tuple-element.205), channel_id=1, source_target_pairs={{0,1},{2,3},{4,5},{6,7},{8,9},{10,11},{12,13},{14,15},{16,17},{18,... | collective-permute-start | bytes 98312 | tf_op jit(solution)/shard_map/ppermute | solution.py:781
  12.9 20.2 %collective-permute-start.1 = (f32[2,8,512]{2,1,0:T(8,128)S(1)}, f32[2,8,512]{2,1,0:T(8,128)S(1)}, u32[]{:S(2)}, u32[]{:S(2)}) collective-permute-start(f32[2,8,512]{2,1,0:T(8,128)S(1)} %get-tuple-element.204), channel_id=1, source_target_pairs={{1,0},{3,2},{5,4},{7,6},{9,8},{11,10},{13,12},{15,14},{17,16},{19,... | collective-permute-start | bytes 98312 | tf_op jit(solution)/shard_map/ppermute | solution.py:781
  14.9 17.5 %collective-permute-start.2 = (f32[2,1280]{1,0:T(2,128)S(1)}, f32[2,1280]{1,0:T(2,128)S(1)}, u32[]{:S(2)}, u32[]{:S(2)}) collective-permute-start(f32[2,1280]{1,0:T(2,128)S(1)} %slice.115), channel_id=1, source_target_pairs={{1,0},{3,2},{5,4},{7,6},{9,8},{11,10},{13,12},{15,14},{17,16},{19,... | collective-permute-start | bytes 30728 | tf_op jit(solution)/shard_map/ppermute | solution.py:781
  16.2 6.2 %copy-start = (bf16[1282,1280]{1,0:T(8,128)(2,1)S(1)}, bf16[1282,1280]{1,0:T(8,128)(2,1)}, u32[]{:S(2)}) copy-start(bf16[1282,1280]{1,0:T(8,128)(2,1)} %constant.165.clone) | copy-start | bytes 9845764
  16.2 6.2 %copy-start.22 = (f32[512,1282]{0,1:T(8,128)S(1)}, f32[512,1282]{0,1:T(8,128)}, u32[]{:S(2)}) copy-start(f32[512,1282]{0,1:T(8,128)} %param.48) | copy-start | bytes 7876612
  22.4 3.5 copy-start.6
  22.4 4.1 %copy-start.12 = (f32[1,1280]{1,0:T(1,128)S(1)}, f32[1,1280]{1,0:T(1,128)}, u32[]{:S(2)}) copy-start(f32[1,1280]{1,0:T(1,128)} %constant.166.clone) | copy-start | bytes 15364
  25.9 4.0 %copy-start.20 = (s32[2]{0:T(128)S(1)}, s32[2]{0:T(128)}, u32[]{:S(2)}) copy-start(s32[2]{0:T(128)} %param.38) | copy-start | bytes 28
  25.9 4.0 %copy-start.21 = (s32[2]{0:T(128)S(1)}, s32[2]{0:T(128)}, u32[]{:S(2)}) copy-start(s32[2]{0:T(128)} %param.37) | copy-start | bytes 28
  25.9 4.6 %copy-start.11 = (f32[1536]{0:T(1024)S(1)}, f32[1536]{0:T(1024)}, u32[]{:S(2)}) copy-start(f32[1536]{0:T(1024)} %param.44) | copy-start | bytes 18436
  33.0 0.6 copy-start.1
  33.1 0.6 copy-start.2
  201.3 26.4 %collective-permute-start.3 = (f32[2,1280]{1,0:T(2,128)S(1)}, f32[2,1280]{1,0:T(2,128)S(1)}, u32[]{:S(2)}, u32[]{:S(2)}) collective-permute-start(f32[2,1280]{1,0:T(2,128)S(1)} %bitcast.58), channel_id=1, source_target_pairs={{0,1},{2,3},{4,5},{6,7},{8,9},{10,11},{12,13},{14,15},{16,17},{18,... | collective-permute-start | bytes 30728 | tf_op jit(solution)/shard_map/ppermute | solution.py:781
  205.8 21.8 %copy-start.13 = (f32[1,1280]{1,0:T(1,128)S(1)}, f32[1,1280]{1,0:T(1,128)}, u32[]{:S(2)}) copy-start(f32[1,1280]{1,0:T(1,128)} %get-tuple-element.155) | copy-start | bytes 15364
  225.1 4.8 %collective-permute-start.4 = (f32[2,8,512]{2,1,0:T(8,128)S(1)}, f32[2,8,512]{2,1,0:T(8,128)S(1)}, u32[]{:S(2)}, u32[]{:S(2)}) collective-permute-start(f32[2,8,512]{2,1,0:T(8,128)S(1)} %get-tuple-element.203), channel_id=1, source_target_pairs={{0,1},{2,3},{4,5},{6,7},{8,9},{10,11},{12,13},{14,15},{16,17},{18,... | collective-permute-start | bytes 98312 | tf_op jit(solution)/shard_map/ppermute | solution.py:781
  226.4 5.8 %collective-permute-start.5 = (f32[2,8,512]{2,1,0:T(8,128)S(1)}, f32[2,8,512]{2,1,0:T(8,128)S(1)}, u32[]{:S(2)}, u32[]{:S(2)}) collective-permute-start(f32[2,8,512]{2,1,0:T(8,128)S(1)} %get-tuple-element.202), channel_id=1, source_target_pairs={{1,0},{3,2},{5,4},{7,6},{9,8},{11,10},{13,12},{15,14},{17,16},{19,... | collective-permute-start | bytes 98312 | tf_op jit(solution)/shard_map/ppermute | solution.py:781
  229.8 2.3 copy-start.3
  232.2 0.6 copy-start.4
  232.8 11.3 %copy-start.5 = (f32[8,512]{1,0:T(8,128)S(1)}, f32[8,512]{1,0:T(8,128)}, u32[]{:S(2)}) copy-start(f32[8,512]{1,0:T(8,128)} %get-tuple-element.154) | copy-start | bytes 49156
  232.8 11.3 %copy-start.9 = (f32[4,512]{1,0:T(4,128)S(1)}, f32[4,512]{1,0:T(4,128)}, u32[]{:S(2)}) copy-start(f32[4,512]{1,0:T(4,128)} %get-tuple-element.140) | copy-start | bytes 24580
  232.8 11.3 %copy-start.10 = (f32[4,512]{1,0:T(4,128)S(1)}, f32[4,512]{1,0:T(4,128)}, u32[]{:S(2)}) copy-start(f32[4,512]{1,0:T(4,128)} %get-tuple-element.141) | copy-start | bytes 24580
  232.8 11.3 %copy-start.14 = (f32[8,1]{1,0:T(8,128)S(1)}, f32[8,1]{1,0:T(8,128)}, u32[]{:S(2)}) copy-start(f32[8,1]{1,0:T(8,128)} %get-tuple-element.156) | copy-start | bytes 100
  232.8 11.3 %copy-start.15 = (f32[1,512]{1,0:T(1,128)S(1)}, f32[1,512]{1,0:T(1,128)}, u32[]{:S(2)}) copy-start(f32[1,512]{1,0:T(1,128)} %get-tuple-element.152) | copy-start | bytes 6148
  232.8 11.3 %copy-start.16 = (f32[1,512]{1,0:T(1,128)S(1)}, f32[1,512]{1,0:T(1,128)}, u32[]{:S(2)}) copy-start(f32[1,512]{1,0:T(1,128)} %get-tuple-element.151) | copy-start | bytes 6148
  232.8 11.3 %copy-start.17 = (f32[1,512]{1,0:T(1,128)S(1)}, f32[1,512]{1,0:T(1,128)}, u32[]{:S(2)}) copy-start(f32[1,512]{1,0:T(1,128)} %get-tuple-element.145) | copy-start | bytes 6148
  232.8 11.3 %copy-start.18 = (f32[1,512]{1,0:T(1,128)S(1)}, f32[1,512]{1,0:T(1,128)}, u32[]{:S(2)}) copy-start(f32[1,512]{1,0:T(1,128)} %get-tuple-element.146) | copy-start | bytes 6148
  232.9 11.3 %copy-start.19 = (f32[1,512]{1,0:T(1,128)S(1)}, f32[1,512]{1,0:T(1,128)}, u32[]{:S(2)}) copy-start(f32[1,512]{1,0:T(1,128)} %get-tuple-element.147) | copy-start | bytes 6148
  232.9 53.4 %copy-start.8 = (f32[512]{0:T(512)S(1)}, f32[512]{0:T(512)}, u32[]{:S(2)}) copy-start(f32[512]{0:T(512)} %param.47) | copy-start | bytes 6148
  291.4 85.9 %copy-start.7 = (f32[1282]{0:T(1024)}, f32[1282]{0:T(1024)S(1)}, u32[]{:S(2)}) copy-start(f32[1282]{0:T(1024)S(1)} %bitcast_dynamic-update-slice_fusion) | copy-start | bytes 15388
  380.8 3.9 copy-start.24
  386.7 1.5 copy-start.23
Sparse Core Ops, SparseCore 0:
  183.1 190.3 all-reduce.6

commit v2 on v1

v2 whole, which is shorter than its diff:
```python
import functools

import jax
import jax.numpy as jnp
import ml_dtypes
import numpy as np
from jax import lax
from jax.experimental import pallas as pl
from jax.experimental.pallas import tpu as pltpu
from jax.sharding import PartitionSpec as P

KERNEL = 7
CLASSES = ((1, 4), (2, 3), (0,))
F32 = jnp.float32
BF16 = jnp.bfloat16
LANES = 128
PAIRS = 128
ROWS = 2 * PAIRS
VMEM = 60 * 2**20
FFN_PARTS = ((1024, 0), (512, 2))
SDS = jax.ShapeDtypeStruct

SIN_POLY = (0.999999996, -0.166666580, 8.33305023e-03, -1.98090119e-04, 2.60507821e-06)
COS_POLY = (1.0, -0.499999994, 4.16666361e-02, -1.38883598e-03, 2.47600798e-05, -2.60500270e-07)

NN = (((1,), (0,)), ((), ()))
NT = (((1,), (1,)), ((), ()))


def split(x):
    high = x.astype(BF16)
    return high, (x - high.astype(F32)).astype(BF16)


def dot(a, b, dims=NN):
    return lax.dot_general(a, b, dims, preferred_element_type=F32)


def dot3(a, b, dims=NN):
    return dot(a[0], b[0], dims) + (dot(a[0], b[1], dims) + dot(a[1], b[0], dims))


def fold8(x):
    return jnp.sum(x.reshape(x.shape[0] // 8, 8, x.shape[1]), axis=0)


def np_split(x):
    high = x.astype(np.float32).astype(ml_dtypes.bfloat16)
    return high, (x - high.astype(np.float64)).astype(ml_dtypes.bfloat16)


@functools.lru_cache(None)
def tables(nfft):
    fifth, half, hop = nfft // 5, nfft // 2, nfft // 4
    bins = np.arange(1, half)
    first, second = (np.concatenate([bins[bins % 5 == r] for r in rs]) for rs in CLASSES[:2])
    zero = np.arange(0, half, 5)
    n0 = np.arange(fifth)

    def paired(ks, residue):
        sign = np.where(ks % 5 == residue, 1.0, -1.0)[:, None]
        turn = 2 * np.pi * ((sign * ks[:, None] * n0[None]) % nfft) / nfft
        weight = 2.0 / nfft
        real = np.concatenate([weight * np.cos(turn), weight * np.sin(turn)], 1)
        imag = np.concatenate([-sign * weight * np.sin(turn), sign * weight * np.cos(turn)], 1)
        return np.concatenate([real, imag], 0)

    turn = 2 * np.pi * ((zero[:, None] * n0[None]) % nfft) / nfft
    weight = np.where(zero == 0, 1.0, 2.0)[:, None] / nfft
    real, imag = weight * np.cos(turn), -weight * np.sin(turn)
    imag[0] = np.cos(np.pi * n0) / nfft
    transforms = [np_split(t) for t in (paired(first, 1), paired(second, 2), np.concatenate([real, imag], 0))]
    n = np.arange(nfft)
    window = 0.5 - 0.5 * np.cos(2 * np.pi * n / nfft)
    windows = np.stack([window, np.roll(window, hop)]).astype(np.float32)
    squares = np.cumsum((window**2).reshape(4, hop), axis=0)
    inverse = np.tile(1.0 / np.maximum(squares, 1.0), (1, 2)).astype(np.float32)
    turns = np.zeros(nfft)
    place = 0
    for ks in (first, second, zero):
        turns[place + len(ks) : place + 2 * len(ks)] = -(np.pi / 2) * (ks % 4)
        place += 2 * len(ks)
    return transforms, windows, inverse, turns.astype(np.float32)[None]


def class_places(nfft):
    length, places, at = nfft // 10, [], 0
    for residues in CLASSES:
        for offset in (0, nfft // 2 + 1):
            for r in residues:
                places.append((at, offset + r))
                at += length
    return places


def sin_cos(x):
    turns = jnp.round(x * np.float32(0.5 / np.pi))
    h = x * 0.5 - turns * np.float32(3.140625)
    h = h - turns * np.float32(9.67502593994140625e-4)
    h = h - turns * np.float32(1.509957990978376432e-7)
    z = h * h
    s = np.float32(SIN_POLY[-1])
    for c in SIN_POLY[-2::-1]:
        s = s * z + np.float32(c)
    s = s * h
    cosine = np.float32(COS_POLY[-1])
    for c in COS_POLY[-2::-1]:
        cosine = cosine * z + np.float32(c)
    twice = s + s
    return twice * cosine, 1.0 - twice * s


def fifths():
    a = 2 * np.pi / 5
    return [np.float32(v) for v in (np.cos(a), np.cos(2 * a), np.sin(a), np.sin(2 * a))]


def inverse_envelope(first_pair, offset, table_ref, tile, rows):
    lane = tile * LANES + lax.broadcasted_iota(jnp.int32, (rows, LANES), 1)
    row = lax.broadcasted_iota(jnp.int32, (rows, LANES), 0)
    half = table_ref.shape[1] // 2
    since = 2 * (first_pair + row) + (lane >= half).astype(jnp.int32) - offset
    value = jnp.where(since < 0, 1.0, 1.0)
    for i in range(4):
        value = jnp.where(since >= i, table_ref[i : i + 1, tile * LANES : (tile + 1) * LANES], value)
    return value


def head_kernel(
    bands,
    offsets,
    x_ref,
    x_up,
    x_down,
    edge_ref,
    cot_ref,
    cot_edge,
    conv_w,
    conv_b,
    scale_t,
    shift_t,
    up_w,
    up_b,
    down_w,
    down_b,
    layer_scale,
    head_wt,
    head_b,
    turns,
    t1h,
    t1l,
    t2h,
    t2l,
    t0h,
    t0l,
    windows,
    inverse,
    o_norm,
    o_istd,
    o_adt_h,
    o_adt_l,
    o_act_h,
    o_act_l,
    o_slope,
    o_spec,
    o_gm,
    o_gb_h,
    o_gb_l,
    o_gbt_h,
    o_gbt_l,
    o_keep,
    o_send,
    o_small,
    up_h,
    up_l,
    down_h,
    down_l,
    head_h,
    head_l,
    head_bias,
    ext_w,
    head4,
    bias4,
    pad4,
    nrm4,
    istd1,
    gs5,
    gm4,
    gl_h,
    gl_l,
    acc_ghw,
    acc_ghb,
    acc_ghwe,
    acc_ghbe,
    acc_gls,
    acc_gmb,
):
    clip, blk = pl.program_id(0), pl.program_id(1)
    clips, blks = pl.num_programs(0), pl.num_programs(1)
    width = x_ref.shape[2]
    frames = blks * ROWS
    tiles = width // LANES
    nfft = turns.shape[1]
    half = nfft // 2
    tm = lax.axis_index("tm")
    band = bands[clip]
    local = offsets[clip] - tm * frames
    rows8 = edge_ref.shape[1]
    places = class_places(nfft)

    @pl.when((clip == 0) & (blk == 0))
    def _():
        up_h[...], up_l[...] = split(up_w[...])
        down_h[...], down_l[...] = split(down_w[...])
        for t in range(tiles):
            head4[t, 0 : nfft + 2, :] = head_wt[:, t * LANES : (t + 1) * LANES]
        bias = head_b[...].reshape(1, nfft + 2)
        for c in range(0, nfft, LANES):
            bias4[c : c + LANES, :] = jnp.broadcast_to(bias[:, c : c + LANES], (LANES, LANES)).T
        for c in (nfft, nfft + 1):
            bias4[c : c + 1, :] = jnp.broadcast_to(bias[:, c : c + 1], (1, LANES))
        for at, first in places:
            rows = jnp.concatenate([head4[t, pl.ds(first, LANES, stride=5), :] for t in range(tiles)], 1)
            head_h[at : at + LANES, :], head_l[at : at + LANES, :] = split(rows)
            moved = bias4[pl.ds(first, LANES, stride=5), :].T[0:1, :]
            head_bias[0:1, at : at + LANES] = moved
            head_bias[1:2, at : at + LANES] = moved + turns[:, at : at + LANES]
        ext_w[0:1, :] = head_wt[half : half + 1, :]
        ext_w[1:2, :] = head_wt[nfft + 1 : nfft + 2, :]
        ext_w[2:8, :] = jnp.zeros((6, width), F32)
        for ref in (acc_ghw, acc_ghb, acc_ghwe, acc_ghbe, acc_gls, acc_gmb):
            ref[...] = jnp.zeros_like(ref)

    base = pl.multiple_of(blk * ROWS, ROWS)

    def masked(value, first):
        row = first + lax.broadcasted_iota(jnp.int32, value.shape, 0)
        return jnp.where(row >= local, value, 0.0)

    before = masked(jnp.where(blk == 0, jnp.where(tm > 0, edge_ref[0], 0.0), x_up[0]), base - rows8)
    after = masked(jnp.where(blk == blks - 1, jnp.where(tm > 0, 0.0, edge_ref[0]), x_down[0]), base + ROWS)
    middle = masked(x_ref[0], base)
    for t in range(tiles):
        lanes = slice(t * LANES, (t + 1) * LANES)
        pad4[t, 0:rows8, :] = before[:, lanes]
        pad4[t, rows8 : rows8 + ROWS, :] = middle[:, lanes]
        pad4[t, rows8 + ROWS :, :] = after[:, lanes]
    bias = conv_b[...].reshape(1, width)
    chunk = 64
    for r in range(0, ROWS, chunk):
        parts = []
        for t in range(tiles):
            lanes = slice(t * LANES, (t + 1) * LANES)
            total = bias[:, lanes]
            for k in range(KERNEL):
                first = r + rows8 - KERNEL // 2 + k
                total = total + pad4[t, first : first + chunk, :] * conv_w[k : k + 1, lanes]
            parts.append(total)
        mean = jnp.sum(sum(parts[1:], parts[0]), axis=1, keepdims=True) * (1.0 / width)
        parts = [p - mean for p in parts]
        squares = [p * p for p in parts]
        variance = jnp.sum(sum(squares[1:], squares[0]), axis=1, keepdims=True) * (1.0 / width)
        istd = lax.rsqrt(variance + 1e-6)
        for t in range(tiles):
            nrm4[t, r : r + chunk, :] = parts[t] * istd
        istd1[r : r + chunk, :] = jnp.broadcast_to(istd, (chunk, LANES))

    def by_parity(ref, first):
        return jnp.concatenate(
            [
                jnp.concatenate([ref[t, pl.ds(first + par, PAIRS, stride=2), :] for t in range(tiles)], 1)
                for par in range(2)
            ],
            0,
        )

    normed = by_parity(nrm4, 0)
    o_norm[...] = normed
    for par in range(2):
        o_istd[par * PAIRS : (par + 1) * PAIRS, :] = istd1[pl.ds(par, PAIRS, stride=2), :]
    adapted = normed * scale_t[pl.ds(band, 1), :] + shift_t[pl.ds(band, 1), :]
    ad = split(adapted)
    o_adt_h[...], o_adt_l[...] = split(adapted.T)

    first_pair = pl.multiple_of(blk * PAIRS, PAIRS)
    wave_tiles = gs5.shape[0]
    pairs = frames // 2
    next_pair = jnp.minimum(first_pair + PAIRS, pairs - 8)
    for t in range(wave_tiles):
        lanes = slice(t * LANES, (t + 1) * LANES)
        stride = clips * wave_tiles
        value = cot_ref[pl.ds(stride * first_pair + clips * t + clip, PAIRS, stride=stride), :]
        gs5[t, 0:PAIRS, :] = value * inverse_envelope(first_pair, local, inverse, t, PAIRS)
        value = cot_ref[pl.ds(stride * next_pair + clips * t + clip, 8, stride=stride), :]
        value = jnp.where(blk == blks - 1, jnp.where(tm > 0, 0.0, cot_edge[0, :, lanes]), value)
        gs5[t, PAIRS : PAIRS + 8, :] = value * inverse_envelope(first_pair + PAIRS, local, inverse, t, 8)
    now, one, two = ([gs5[t, d : d + PAIRS, :] for t in range(wave_tiles)] for d in range(3))
    mid = wave_tiles // 2
    right = lax.broadcasted_iota(jnp.int32, (PAIRS, LANES), 1) >= LANES // 2
    odd = two[:mid] + [jnp.where(right, now[mid], two[mid])] + now[mid + 1 :] + one
    c1, c2, s1, s2 = fifths()
    folded = []
    for par, segment in enumerate((now + one, odd)):
        seg = [v * windows[par : par + 1, t * LANES : (t + 1) * LANES] for t, v in enumerate(segment)]
        v = [jnp.concatenate(seg[2 * j : 2 * j + 2], 1) for j in range(5)]
        p14, m41, p23, m32 = v[1] + v[4], v[4] - v[1], v[2] + v[3], v[3] - v[2]
        folded.append(
            (
                v[0] + p14 + p23,
                v[0] + c1 * p14 + c2 * p23,
                s1 * m41 + s2 * m32,
                v[0] + c2 * p14 + c1 * p23,
                s2 * m41 - s1 * m32,
            )
        )
    f0, fa, fb, fc, fd = (jnp.concatenate([e, o], 0) for e, o in zip(*folded))
    spectrum_grads = (
        dot3(split(jnp.concatenate([fa, fb], 1)), (t1h[...], t1l[...]), NT),
        dot3(split(jnp.concatenate([fc, fd], 1)), (t2h[...], t2l[...]), NT),
        dot3(split(f0), (t0h[...], t0l[...]), NT),
    )

    hidden = up_h.shape[1]
    step = 256
    up_bias = up_b[...].reshape(1, hidden)
    for j in range(hidden // step):
        cols = slice(j * step, (j + 1) * step)
        upward = dot3(ad, (up_h[:, cols], up_l[:, cols])) + up_bias[:, cols]
        cdf = 0.5 + 0.5 * lax.erf(upward * np.float32(0.7071067811865476))
        density = jnp.exp(upward * upward * -0.5) * np.float32(0.3989422804014327)
        o_slope[:, cols] = cdf + upward * density
        o_act_h[:, cols], o_act_l[:, cols] = split(upward * cdf)
    branch = dot3((o_act_h[...], o_act_l[...]), (down_h[...], down_l[...])) + down_b[...].reshape(1, width)
    scale = layer_scale[...].reshape(1, width)
    residual = by_parity(pad4, rows8) + scale * branch
    res = split(residual)
    res_t = split(residual.T)

    bias = head_b[...].reshape(1, nfft + 2)
    ext = split(ext_w[...])
    ext_logits = dot3(ext, res, NT)
    lane = lax.broadcasted_iota(jnp.int32, (1, ROWS), 1)
    ext_frame = base + jnp.where(lane < PAIRS, 2 * lane, 2 * (lane - PAIRS) + 1)
    ext_present = ext_frame >= local

    def magnitudes(logits, present):
        raw = jnp.where(present, jnp.exp(logits), 0.0)
        squashed = jnp.tanh(raw * np.float32(0.01))
        return 100.0 * squashed, raw * (1.0 - squashed * squashed)

    ext_mag, ext_slope = magnitudes(ext_logits[0:1] + bias[:, half : half + 1], ext_present)
    ext_sin, ext_cos = sin_cos(ext_logits[1:2] + bias[:, nfft + 1 : nfft + 2])
    ext_real = ext_mag * ext_cos
    ext_imag = ext_mag * ext_sin
    ext_real_col = jnp.concatenate([ext_real, jnp.zeros((7, ROWS), F32)], 0).T[:, 0:1]

    row = lax.broadcasted_iota(jnp.int32, (PAIRS, 1), 0)
    at = 0
    for index, grads in enumerate(spectrum_grads):
        n = grads.shape[1] // 2
        cols = slice(at, at + 2 * n)
        logits = dot3(res, (head_h[cols, :], head_l[cols, :]), NT)
        for par in range(2):
            rows = slice(par * PAIRS, (par + 1) * PAIRS)
            present = base + 2 * row + par >= local
            value = logits[rows] + head_bias[par : par + 1, cols]
            magnitude, slope = magnitudes(value[:, :n], present)
            sine, cosine = sin_cos(value[:, n:])
            real, imag = magnitude * cosine, magnitude * sine
            g_real, g_imag = grads[rows, :n], grads[rows, n:]
            if index == 2:
                corner = lax.broadcasted_iota(jnp.int32, (PAIRS, n), 1) == 0
                shown = jnp.where(corner, ext_real_col[rows], imag)
                g_imag = jnp.where(corner, 0.0, g_imag)
            else:
                shown = imag
            o_spec[rows, at : at + n] = real
            o_spec[rows, at + n : at + 2 * n] = shown
            g_mag = slope * (g_real * cosine + g_imag * sine)
            g_ang = g_imag * real - g_real * imag
            gl = jnp.concatenate([g_mag, g_ang], 1)
            acc_ghb[:, cols] += fold8(gl)
            gl_h[rows, cols], gl_l[rows, cols] = split(gl)
        at += 2 * n

    corner_t = spectrum_grads[2][:, spectrum_grads[2].shape[1] // 2 :].T
    ext_g = corner_t[0:1, :]
    ext_grads = jnp.concatenate(
        [ext_slope * ext_g * ext_cos, -ext_g * ext_imag, jnp.zeros((6, ROWS), F32)], 0
    )
    acc_ghbe[...] += ext_grads
    acc_ghwe[...] += dot3(split(ext_grads), res)
    gl = (gl_h[...], gl_l[...])
    ext_cols = ext_grads.T
    grad_mixed = (
        dot3(gl, (head_h[...], head_l[...]))
        + ext_cols[:, 0:1] * ext_w[0:1, :]
        + ext_cols[:, 1:2] * ext_w[1:2, :]
    )
    acc_ghw[...] += dot3(res_t, gl)
    acc_gls[...] += fold8(grad_mixed * branch)
    acc_gmb[...] += fold8(grad_mixed)
    for par in range(2):
        rows = slice(par * PAIRS, (par + 1) * PAIRS)
        for t in range(tiles):
            gm4[t, pl.ds(par, PAIRS, stride=2), :] = grad_mixed[rows, t * LANES : (t + 1) * LANES]
    for t in range(tiles):
        o_gm[:, t * LANES : (t + 1) * LANES] = gm4[t]
    grad_branch = grad_mixed * scale
    o_gb_h[...], o_gb_l[...] = split(grad_branch)
    o_gbt_h[...], o_gbt_l[...] = split(grad_branch.T)

    @pl.when((clip == clips - 1) & (blk == blks - 1))
    def _():
        total = jnp.sum(acc_ghb[...], axis=0, keepdims=True)
        for at, first in places:
            for t in range(tiles):
                block = acc_ghw[t * LANES : (t + 1) * LANES, at : at + LANES]
                head4[t, pl.ds(first, LANES, stride=5), :] = block.T
            block = jnp.broadcast_to(total[:, at : at + LANES], (LANES, LANES))
            bias4[pl.ds(first, LANES, stride=5), :] = block.T
        ext_sums = jnp.sum(acc_ghbe[...], axis=1, keepdims=True)
        for i, c in enumerate((half, nfft + 1)):
            for t in range(tiles):
                head4[t, c : c + 1, :] = acc_ghwe[i : i + 1, t * LANES : (t + 1) * LANES]
            bias4[c : c + 1, :] = jnp.broadcast_to(ext_sums[i : i + 1], (1, LANES))
        core = lax.axis_index("clip") % 2
        rows = o_keep.shape[0]
        for t in range(tiles):
            head4[t, nfft + 2 :, :] = jnp.zeros((2 * rows - nfft - 2, LANES), F32)
            for ref, part in ((o_keep, core), (o_send, 1 - core)):
                mine = pl.ds(pl.multiple_of(part * rows, rows), rows)
                ref[:, t * LANES : (t + 1) * LANES] = head4[t, mine, :]
        o_small[...] = jnp.zeros_like(o_small)
        for c in range(0, nfft, LANES):
            o_small[0:1, c : c + LANES] = bias4[c : c + LANES, :].T[0:1, :]
        o_small[0:1, nfft : nfft + 2] = jnp.concatenate(
            [bias4[nfft : nfft + 1, 0:1], bias4[nfft + 1 : nfft + 2, 0:1]], 1
        )
        o_small[1:2, :width] = jnp.sum(acc_gls[...], axis=0, keepdims=True)
        o_small[2:3, :width] = jnp.sum(acc_gmb[...], axis=0, keepdims=True) * scale


def whole(shape):
    return pl.BlockSpec(shape, lambda *_: (0,) * len(shape))


def fixed(shape):
    return pl.BlockSpec(shape, lambda *_: (0,) * len(shape), pipeline_mode=pl.Buffered(1))


def row_halves(blks, rows, rows8, width, clip=None):
    per, last = rows // rows8, blks * rows // rows8 - 1
    places = [
        (rows, lambda j: j),
        (rows8, lambda j: jnp.maximum(j * per - 1, 0)),
        (rows8, lambda j: jnp.minimum(j * per + per, last)),
    ]
    if clip is None:
        return [pl.BlockSpec((1, n, width), lambda i, j, *_, f=f: (i, f(j), 0)) for n, f in places]
    return [pl.BlockSpec((1, n, width), lambda j, *_, f=f: (clip, f(j), 0)) for n, f in places]


def run_head(bands, offsets, x, edge, cot, cot_edge, weights, turns, consts):
    clips, frames, width = x.shape
    blks = frames // ROWS
    count = clips * frames
    hidden = weights[4].shape[1]
    nfft = turns.shape[1]
    block = lambda i, j, *_: (i * blks + j, 0)
    column = lambda i, j, *_: (0, i * blks + j)
    per_clip = lambda shape: pl.BlockSpec((1,) + shape, lambda i, j, *_: (i, 0, 0))
    in_specs = row_halves(blks, ROWS, edge.shape[1], width)
    in_specs += [per_clip(edge.shape[1:])]
    operands = list(weights) + [turns] + list(consts)
    in_specs += [fixed(cot.shape), per_clip(cot_edge.shape[1:])] + [fixed(v.shape) for v in operands]
    padded = -(-(nfft + 2) // 64) * 64
    row_out = lambda n, dtype: (SDS((count, n), dtype), pl.BlockSpec((ROWS, n), block))
    col_out = (SDS((width, count), BF16), pl.BlockSpec((width, ROWS), column))
    outs = [
        row_out(width, F32),
        row_out(LANES, F32),
        col_out,
        col_out,
        row_out(hidden, BF16),
        row_out(hidden, BF16),
        row_out(hidden, F32),
        row_out(nfft, F32),
        row_out(width, F32),
        row_out(width, BF16),
        row_out(width, BF16),
        col_out,
        col_out,
        (SDS((padded // 2, width), F32), whole((padded // 2, width))),
        (SDS((padded // 2, width), F32), whole((padded // 2, width))),
        (SDS((8, hidden), F32), whole((8, hidden))),
    ]
    wave_tiles = nfft // 2 // LANES
    tiles = width // LANES
    scratch = [pltpu.VMEM((width, hidden), BF16)] * 2 + [pltpu.VMEM((hidden, width), BF16)] * 2
    scratch += [
        pltpu.VMEM((nfft, width), BF16),
        pltpu.VMEM((nfft, width), BF16),
        pltpu.VMEM((2, nfft), F32),
        pltpu.VMEM((8, width), F32),
        pltpu.VMEM((tiles, padded, LANES), F32),
        pltpu.VMEM((nfft + 8, LANES), F32),
        pltpu.VMEM((tiles, ROWS + 2 * edge.shape[1], LANES), F32),
        pltpu.VMEM((tiles, ROWS, LANES), F32),
        pltpu.VMEM((ROWS, LANES), F32),
        pltpu.VMEM((wave_tiles, PAIRS + 8, LANES), F32),
        pltpu.VMEM((tiles, ROWS, LANES), F32),
        pltpu.VMEM((ROWS, nfft), BF16),
        pltpu.VMEM((ROWS, nfft), BF16),
        pltpu.VMEM((width, nfft), F32),
        pltpu.VMEM((8, nfft), F32),
        pltpu.VMEM((8, width), F32),
        pltpu.VMEM((8, ROWS), F32),
        pltpu.VMEM((8, width), F32),
        pltpu.VMEM((8, width), F32),
    ]
    return pl.pallas_call(
        head_kernel,
        grid_spec=pltpu.PrefetchScalarGridSpec(
            num_scalar_prefetch=2,
            grid=(clips, blks),
            in_specs=in_specs,
            out_specs=[s for _, s in outs],
            scratch_shapes=scratch,
        ),
        out_shape=[s for s, _ in outs],
        compiler_params=pltpu.CompilerParams(vmem_limit_bytes=VMEM),
        cost_estimate=pl.CostEstimate(flops=80_000_000_000, bytes_accessed=90_000_000, transcendentals=0),
        name="head",
    )(bands, offsets, x, x, x, edge, cot, cot_edge, *operands)


def ffn_kernel(
    gb_h, gb_l, gbt_h, gbt_l, act_h, act_l, slope, adt_h, adt_l, down_w, *refs
):
    o_keep, o_send, o_gub, o_gu_h, o_gu_l, dw_h, dw_l, acc_gdn, acc_gup, acc_gub = refs[-10:]
    step = pl.program_id(0)
    hidden, width = down_w.shape

    @pl.when(step == 0)
    def _():
        dw_h[...], dw_l[...] = split(down_w[...])
        for ref in (acc_gdn, acc_gup, acc_gub):
            ref[...] = jnp.zeros_like(ref)

    acc_gdn[...] += dot3((gbt_h[...], gbt_l[...]), (act_h[...], act_l[...]))
    cols = 256
    for j in range(hidden // cols):
        part = slice(j * cols, (j + 1) * cols)
        gu = dot3((gb_h[...], gb_l[...]), (dw_h[part, :], dw_l[part, :]), NT) * slope[:, part]
        acc_gub[:, part] += fold8(gu)
        gs = split(gu)
        o_gu_h[:, part], o_gu_l[:, part] = gs
        acc_gup[:, part] += dot3((adt_h[...], adt_l[...]), gs)

    @pl.when(step == pl.num_programs(0) - 1)
    def _():
        o_gub[...] = jnp.sum(acc_gub[...], axis=0, keepdims=True)
        core = lax.axis_index("clip") % 2
        rows = hidden // 2
        for ref, half in ((o_keep, core), (o_send, 1 - core)):
            mine = pl.ds(pl.multiple_of(half * rows, rows), rows)
            ref[0:rows, :] = acc_gdn[:, mine].T
            ref[rows:, :] = acc_gup[:, mine].T


def after(values):
    return [pl.BlockSpec(memory_space=pl.ANY)] * len(values), list(values)


def run_ffn(gb, gbt, act, slope, adt, down_w, hidden, part, waits=()):
    count, width = gb[0].shape
    rows = 512
    row = lambda i, *_: (i, 0)
    mine = lambda i, *_: (i, part)
    col = lambda i, *_: (0, i)
    in_specs = [pl.BlockSpec((rows, width), row)] * 2 + [pl.BlockSpec((width, rows), col)] * 2
    in_specs += [pl.BlockSpec((rows, hidden), mine)] * 3 + [pl.BlockSpec((width, rows), col)] * 2
    in_specs += [pl.BlockSpec((hidden, width), lambda i, *_: (part, 0), pipeline_mode=pl.Buffered(1))]
    wait_specs, waits = after(waits)
    return pl.pallas_call(
        ffn_kernel,
        grid=(count // rows,),
        in_specs=in_specs + wait_specs,
        out_specs=[
            whole((hidden, width)),
            whole((hidden, width)),
            whole((1, hidden)),
            pl.BlockSpec((rows, hidden), row),
            pl.BlockSpec((rows, hidden), row),
        ],
        out_shape=[
            SDS((hidden, width), F32),
            SDS((hidden, width), F32),
            SDS((1, hidden), F32),
            SDS((count, hidden), BF16),
            SDS((count, hidden), BF16),
        ],
        scratch_shapes=[pltpu.VMEM((hidden, width), BF16)] * 2
        + [pltpu.VMEM((width, hidden), F32)] * 2
        + [pltpu.VMEM((8, hidden), F32)],
        compiler_params=pltpu.CompilerParams(vmem_limit_bytes=VMEM),
        cost_estimate=pl.CostEstimate(
            flops=18 * count * width * hidden, bytes_accessed=12 * count * hidden, transcendentals=0
        ),
        name="ffn_grads",
    )(*gb, *gbt, *act, slope, *adt, down_w, *waits)


def norm_kernel(sizes, clip, bands, *refs):
    gu = refs[: 2 * len(sizes)]
    up_w, norm, istd, scale_t = refs[2 * len(sizes) : 2 * len(sizes) + 4]
    o_gh, o_scale, o_shift, up_h, up_l, nat4, acc_scale, acc_shift = refs[-8:]
    blk, blks = pl.program_id(0), pl.num_programs(0)
    band = bands[clip]
    width = norm.shape[1]
    tiles = width // LANES

    @pl.when(blk == 0)
    def _():
        up_h[...], up_l[...] = split(up_w[...])
        for ref in (o_scale, o_shift, acc_scale, acc_shift):
            ref[...] = jnp.zeros_like(ref)

    ga, at = None, 0
    for j, hidden in enumerate(sizes):
        cols = slice(at, at + hidden)
        term = dot3((gu[2 * j][...], gu[2 * j + 1][...]), (up_h[:, cols], up_l[:, cols]), NT)
        ga = term if ga is None else ga + term
        at += hidden
    normed = norm[...]
    acc_scale[...] += fold8(ga * normed)
    acc_shift[...] += fold8(ga)
    gn = ga * scale_t[pl.ds(band, 1), :]
    mean = jnp.sum(gn, axis=1, keepdims=True) * (1.0 / width)
    along = jnp.sum(gn * normed, axis=1, keepdims=True) * (1.0 / width)
    gh = istd[:, 0:1] * (gn - mean - normed * along)
    for par in range(2):
        for t in range(tiles):
            nat4[t, pl.ds(par, PAIRS, stride=2), :] = gh[par * PAIRS : (par + 1) * PAIRS, t * LANES : (t + 1) * LANES]
    for t in range(tiles):
        o_gh[:, t * LANES : (t + 1) * LANES] = nat4[t]

    @pl.when(blk == blks - 1)
    def _():
        o_scale[pl.ds(band, 1), :] = jnp.sum(acc_scale[...], axis=0, keepdims=True)
        o_shift[pl.ds(band, 1), :] = jnp.sum(acc_shift[...], axis=0, keepdims=True)


def run_norm(bands, gus, up_w, norm, istd, scale_t, clips, clip, waits=()):
    count, width = norm.shape
    blks = count // clips // ROWS
    block = lambda j, *_: (clip * blks + j, 0)
    flat = [v for pair in gus for v in pair]
    in_specs = [pl.BlockSpec((ROWS, v.shape[1]), block) for v in flat]
    in_specs += [fixed(up_w.shape), pl.BlockSpec((ROWS, width), block)]
    in_specs += [pl.BlockSpec((ROWS, LANES), block), fixed(scale_t.shape)]
    wait_specs, waits = after(waits)
    return pl.pallas_call(
        functools.partial(norm_kernel, [pair[0].shape[1] for pair in gus], clip),
        grid_spec=pltpu.PrefetchScalarGridSpec(
            num_scalar_prefetch=1,
            grid=(blks,),
            in_specs=in_specs + wait_specs,
            out_specs=[pl.BlockSpec((ROWS, width), lambda j, *_: (j, 0)), whole(scale_t.shape), whole(scale_t.shape)],
            scratch_shapes=[pltpu.VMEM(up_w.shape, BF16)] * 2
            + [pltpu.VMEM((width // LANES, ROWS, LANES), F32)]
            + [pltpu.VMEM((8, width), F32)] * 2,
        ),
        out_shape=[SDS((count // clips, width), F32), SDS(scale_t.shape, F32), SDS(scale_t.shape, F32)],
        compiler_params=pltpu.CompilerParams(vmem_limit_bytes=VMEM),
        cost_estimate=pl.CostEstimate(flops=5_000_000_000, bytes_accessed=12_000_000, transcendentals=0),
        name="norm_grads",
    )(bands, *flat, up_w, norm, istd, scale_t, *waits)


def conv_kernel(
    clip, offsets, x_ref, x_up, x_down, edge_ref, gh_ref, gh_up, gh_down, gh_edge, gm_ref, conv_w, acc_in, *refs
):
    o_gi, o_acc, pad4, gh4 = refs[-4:]
    blk, blks = pl.program_id(0), pl.num_programs(0)
    rows, width = x_ref.shape[1], x_ref.shape[2]
    tiles = width // LANES
    tm = lax.axis_index("tm")
    local = offsets[clip] - tm * blks * rows
    rows8 = edge_ref.shape[1]
    base = blk * rows

    @pl.when(blk == 0)
    def _():
        o_acc[...] = acc_in[...]

    def masked(value, first):
        row = first + lax.broadcasted_iota(jnp.int32, value.shape, 0)
        return jnp.where(row >= local, value, 0.0)

    def above(edge, up):
        return jnp.where(blk == 0, jnp.where(tm > 0, edge[0], 0.0), up[0])

    def below(edge, down):
        return jnp.where(blk == blks - 1, jnp.where(tm > 0, 0.0, edge[0]), down[0])

    before, after = masked(above(edge_ref, x_up), base - rows8), masked(below(edge_ref, x_down), base + rows)
    g_before, g_after = above(gh_edge, gh_up), below(gh_edge, gh_down)
    middle = masked(x_ref[0], base)
    for t in range(tiles):
        lanes = slice(t * LANES, (t + 1) * LANES)
        pad4[t, 0:rows8, :] = before[:, lanes]
        pad4[t, rows8 : rows8 + rows, :] = middle[:, lanes]
        pad4[t, rows8 + rows :, :] = after[:, lanes]
        gh4[t, 0:rows8, :] = g_before[:, lanes]
        gh4[t, rows8 : rows8 + rows, :] = gh_ref[0, :, lanes]
        gh4[t, rows8 + rows :, :] = g_after[:, lanes]
    chunk = 64
    for r in range(0, rows, chunk):
        shown = base + r + lax.broadcasted_iota(jnp.int32, (chunk, LANES), 0) >= local
        for t in range(tiles):
            lanes = slice(t * LANES, (t + 1) * LANES)
            gh = gh4[t, rows8 + r : rows8 + r + chunk, :]
            o_acc[8 * KERNEL :, lanes] += fold8(gh)
            total = gm_ref[0, r : r + chunk, lanes]
            for k in range(KERNEL):
                first = r + rows8 + KERNEL // 2 - k
                total = total + conv_w[k : k + 1, lanes] * gh4[t, first : first + chunk, :]
                first = r + rows8 - KERNEL // 2 + k
                o_acc[8 * k : 8 * k + 8, lanes] += fold8(gh * pad4[t, first : first + chunk, :])
            o_gi[0, r : r + chunk, lanes] = jnp.where(shown, total, 0.0)


def run_conv(offsets, x, edge, gh, gh_edge, gm, conv_w, clip, so_far, waits=()):
    clips, frames, width = x.shape
    blks = frames // ROWS
    rows8 = edge.shape[1]
    mine = pl.BlockSpec((1, rows8, width), lambda j, *_: (clip, 0, 0))
    padded = pltpu.VMEM((width // LANES, ROWS + 2 * rows8, LANES), F32)
    blocks = row_halves(blks, ROWS, rows8, width, clip)
    in_specs = blocks + [mine] + row_halves(blks, ROWS, rows8, width, 0) + [mine] + blocks[:1]
    grads, acc = so_far
    in_specs += [fixed(conv_w.shape), fixed(acc.shape)]
    operands = [x, x, x, edge, gh, gh, gh, gh_edge, gm, conv_w, acc]
    aliases = {}
    wait_specs, waits = after(waits)
    if grads is not None:
        aliases = {1 + len(operands): 0}
        operands.append(grads)
        in_specs.append(pl.BlockSpec(memory_space=pl.ANY))
    return pl.pallas_call(
        functools.partial(conv_kernel, clip),
        grid_spec=pltpu.PrefetchScalarGridSpec(
            num_scalar_prefetch=1,
            grid=(blks,),
            in_specs=in_specs + wait_specs,
            out_specs=[blocks[0], whole(acc.shape)],
            scratch_shapes=[padded, padded],
        ),
        out_shape=[SDS(x.shape, F32), SDS(acc.shape, F32)],
        input_output_aliases=aliases,
        compiler_params=pltpu.CompilerParams(vmem_limit_bytes=VMEM),
        cost_estimate=pl.CostEstimate(flops=5_000_000_000, bytes_accessed=17_000_000, transcendentals=0),
        name="conv_grads",
    )(offsets, *operands, *waits)


def pack_kernel(acc, small, scales0, scales1, shifts0, shifts1, *refs):
    gubs, o_pack = refs[:-1], refs[-1]
    width = acc.shape[1]
    for k in range(KERNEL + 1):
        o_pack[k : k + 1, :] = jnp.sum(acc[8 * k : 8 * k + 8, :], axis=0, keepdims=True)
    o_pack[8:12, :] = scales0[...] + scales1[...]
    o_pack[12:16, :] = shifts0[...] + shifts1[...]
    o_pack[16:18, :] = small[1:3, :width]
    for i in range(3):
        o_pack[18 + i : 19 + i, :] = small[0:1, i * width : (i + 1) * width]
        gub = jnp.concatenate([v[...] for v in gubs], 1)
        o_pack[21 + i : 22 + i, :] = gub[:, i * width : (i + 1) * width]
    o_pack[24:, :] = jnp.zeros((o_pack.shape[0] - 24, width), F32)


def wave_kernel(
    first_blk, frames, offsets, spec, carry, t1h, t1l, t2h, t2l, t0h, t0l, windows, inverse, *refs
):
    o_wave, o_tail, accs = refs[-3:]
    blk, clip = pl.program_id(0), pl.program_id(1)
    blks, clips = pl.num_programs(0), pl.num_programs(1)
    tiles = accs.shape[1]
    first = (first_blk + blk) * PAIRS
    local = offsets[clip] - lax.axis_index("tm") * frames
    acc5 = accs.at[clip]

    @pl.when(blk == 0)
    def _():
        for t in range(tiles):
            acc5[t, 0:8, :] = carry[0, :, t * LANES : (t + 1) * LANES]

    @pl.when(blk > 0)
    def _():
        for t in range(tiles):
            acc5[t, 0:8, :] = acc5[t, PAIRS : PAIRS + 8, :]

    for t in range(tiles):
        acc5[t, 8:, :] = jnp.zeros((PAIRS, LANES), F32)

    n1, n2 = t1h.shape[0], t2h.shape[0]
    ab = dot3(split(spec[:, :n1]), (t1h[...], t1l[...]))
    cd = dot3(split(spec[:, n1 : n1 + n2]), (t2h[...], t2l[...]))
    p0 = dot3(split(spec[:, n1 + n2 :]), (t0h[...], t0l[...]))
    c1, c2, s1, s2 = fifths()
    sides = []
    for par in range(2):
        rows = slice(par * PAIRS, (par + 1) * PAIRS)
        w = p0.shape[1]
        a, b, c, d, p = ab[rows, :w], ab[rows, w:], cd[rows, :w], cd[rows, w:], p0[rows]
        e1, o1 = p + c1 * a + c2 * c, s1 * b + s2 * d
        e2, o2 = p + c2 * a + c1 * c, s2 * b - s1 * d
        v = [p + a + c, e1 - o1, e2 - o2, e2 + o2, e1 + o1]
        seg = []
        for t in range(2 * tiles):
            part = v[t // 2][:, (t % 2) * LANES : (t % 2 + 1) * LANES]
            seg.append(part * windows[par : par + 1, t * LANES : (t + 1) * LANES])
        sides.append(seg)
    even, odd = sides
    mid = tiles // 2
    right = lax.broadcasted_iota(jnp.int32, (PAIRS, LANES), 1) >= LANES // 2
    for t in range(tiles):
        here = even[t]
        if t > mid:
            here = here + odd[t]
        if t == mid:
            here = here + jnp.where(right, odd[t], 0.0)
        acc5[t, 0:PAIRS, :] += here
        acc5[t, 1 : PAIRS + 1, :] += even[tiles + t] + odd[tiles + t]
        if t < mid:
            acc5[t, 2 : PAIRS + 2, :] += odd[t]
        if t == mid:
            acc5[t, 2 : PAIRS + 2, :] += jnp.where(right, 0.0, odd[t])
        value = acc5[t, 0:PAIRS, :] * inverse_envelope(first, local, inverse, t, PAIRS)
        o_wave[pl.ds(clips * t + clip, PAIRS, stride=clips * tiles), :] = value

    @pl.when(blk == blks - 1)
    def _():
        for t in range(tiles):
            o_tail[0, :, t * LANES : (t + 1) * LANES] = acc5[t, PAIRS : PAIRS + 8, :]


def run_wave(offsets, spec, consts, clips, first_blk, blks, carry, wave=None, waits=()):
    count, nfft = spec.shape
    all_blks = count // clips // ROWS
    tiles = nfft // 2 // LANES
    rows = clips * PAIRS * tiles
    in_specs = [pl.BlockSpec((ROWS, nfft), lambda j, i, *_: (i * all_blks + first_blk + j, 0))]
    in_specs += [pl.BlockSpec((1, 8, nfft // 2), lambda j, i, *_: (i, 0, 0))]
    in_specs += [fixed(v.shape) for v in consts]
    operands = [spec, carry, *consts]
    aliases = {}
    wait_specs, waits = after(waits)
    if wave is not None:
        aliases = {1 + len(operands): 0}
        operands.append(wave)
        in_specs.append(pl.BlockSpec(memory_space=pl.ANY))
    return pl.pallas_call(
        functools.partial(wave_kernel, first_blk, count // clips),
        grid_spec=pltpu.PrefetchScalarGridSpec(
            num_scalar_prefetch=1,
            grid=(blks, clips),
            in_specs=in_specs + wait_specs,
            out_specs=[
                pl.BlockSpec((rows, LANES), lambda j, i, *_: (first_blk + j, 0)),
                pl.BlockSpec((1, 8, nfft // 2), lambda j, i, *_: (i, 0, 0)),
            ],
            scratch_shapes=[pltpu.VMEM((clips, tiles, PAIRS + 8, LANES), F32)],
        ),
        out_shape=[SDS((rows * all_blks, LANES), F32), SDS((clips, 8, nfft // 2), F32)],
        input_output_aliases=aliases,
        compiler_params=pltpu.CompilerParams(vmem_limit_bytes=VMEM),
        cost_estimate=pl.CostEstimate(flops=5_000_000_000, bytes_accessed=8_000_000, transcendentals=0),
        name="wave",
    )(offsets, *operands, *waits)


def levels():
    clip = [("clip", 1 << i) for i in range((lax.axis_size("clip") - 1).bit_length())]
    tm = [("tm", 1 << i) for i in range((lax.axis_size("tm") - 1).bit_length())]
    return clip[:1] + clip[1:2] + tm + clip[2:]


def exchange(value, level):
    axis, distance = level
    return lax.ppermute(value, axis, [(i, i ^ distance) for i in range(lax.axis_size(axis))])


def side(level):
    axis, distance = level
    return lax.axis_index(axis) // distance % 2


class Sums:
    def __init__(self):
        self.running = []

    def add(self, steps, holds=()):
        entry = {"steps": steps, "holds": holds, "count": 0, "sent": None, "came": None, "left": 0, "sum": None}
        self.step(entry, None)
        self.running.append(entry)
        return entry

    def step(self, entry, value):
        try:
            entry["sent"] = entry["steps"].send(value)
            while entry["sent"][1] == levels()[0]:
                entry["sent"] = entry["steps"].send(exchange(*entry["sent"]))
        except StopIteration as stop:
            entry["sent"], entry["sum"] = None, stop.value

    def waits(self):
        sent = []
        for entry in self.running:
            if entry["came"] is None and entry["sent"] is not None:
                entry["came"] = exchange(*entry["sent"])
                entry["left"] = dict(entry["holds"]).get(entry["count"], 1)
                entry["count"] += 1
                sent.append(entry["sent"][0])
        return sent

    def advance(self, results):
        done = []
        for entry in self.running:
            if entry["came"] is not None:
                entry["left"] -= 1
                if entry["left"] <= 0:
                    done.append(entry)
        if done:
            came, results = lax.optimization_barrier(([entry["came"] for entry in done], results))
            for entry, value in zip(done, came):
                entry["came"] = None
                self.step(entry, value)
        return results

    def finish(self, entry):
        while entry["sum"] is None:
            self.waits()
            self.advance(())
        return entry["sum"]


def halves_steps(keep, send, turn):
    core, *rest = levels()
    first, last = rest[:2], rest[2:]
    if turn % 2:
        first = first[::-1]
    value = keep + (yield send, core)
    for level in first:
        rows, s = value.shape[0] // 2, side(level)
        away = lax.dynamic_slice_in_dim(value, (1 - s) * rows, rows)
        value = lax.dynamic_slice_in_dim(value, s * rows, rows) + (yield away, level)
    for level in last:
        value = value + (yield value, level)
    for level in first[::-1]:
        value = jnp.concatenate([value, (yield value, level)])
    other = yield value, core
    return value, other, [core, *first]


def whole_steps(value):
    for level in levels():
        value = value + (yield value, level)
    return value


def natural_blocks(order, mine, other, copy):
    s = [side(level) for level in order]
    rows = mine.shape[0] // 4
    for half in range(2):
        for ref, here in ((mine, s[0] == half), (other, s[0] != half)):

            @pl.when(here)
            def _(ref=ref, half=half):
                for a in range(2):
                    for b in range(2):
                        first = (2 * jnp.bitwise_xor(a, s[1]) + jnp.bitwise_xor(b, s[2])) * rows
                        copy(half, a, b, ref[pl.ds(pl.multiple_of(first, 8), rows), :])


def head_order_kernel(order, mine, other, *refs):
    out = refs[-1]

    def copy(half, a, b, block):
        rows = block.shape[0]
        first = ((2 * half + a) * 2 + b) * rows
        end = min(first + rows, out.shape[0])
        out[first:end, :] = block[: end - first]

    natural_blocks(order, mine, other, copy)


def ffn_order_kernel(order, mine, other, *refs):
    o_down, o_up, up_t = refs[-3:]

    def copy(half, a, b, block):
        rows = block.shape[0]
        first = (2 * half + b) * rows
        (up_t if a else o_down)[first : first + rows, :] = block

    natural_blocks(order, mine, other, copy)
    for c in range(0, up_t.shape[0], LANES):
        o_up[:, c : c + LANES] = up_t[c : c + LANES, :].T


def order_head(total, rows, waits=()):
    mine, other, order = total
    wait_specs, waits = after(waits)
    return pl.pallas_call(
        functools.partial(head_order_kernel, order),
        in_specs=[pl.BlockSpec(memory_space=pltpu.VMEM)] * 2 + wait_specs,
        out_shape=SDS((rows, mine.shape[1]), F32),
        compiler_params=pltpu.CompilerParams(vmem_limit_bytes=VMEM),
        name="head_order",
    )(mine, other, *waits)


def order_ffn(total, hidden, part, so_far, waits=()):
    mine, other, order = total
    size, width = mine.shape[0], mine.shape[1]
    so_far = list(so_far)
    wait_specs, waits = after(waits)
    return pl.pallas_call(
        functools.partial(ffn_order_kernel, order),
        grid=(1,),
        in_specs=[whole(mine.shape)] * 2 + [pl.BlockSpec(memory_space=pl.ANY)] * len(so_far) + wait_specs,
        out_specs=[
            pl.BlockSpec((size, width), lambda i: (part, 0)),
            pl.BlockSpec((width, size), lambda i: (0, part)),
        ],
        out_shape=[SDS((hidden, width), F32), SDS((width, hidden), F32)],
        scratch_shapes=[pltpu.VMEM((size, width), F32)],
        input_output_aliases={2 + i: i for i in range(len(so_far))},
        compiler_params=pltpu.CompilerParams(vmem_limit_bytes=VMEM),
        name="ffn_order",
    )(mine, other, *so_far, *waits)


def unpack_kernel(pack, gcw, gcb, gscale, gshift, gls, gdb, ghb, gub):
    width = pack.shape[1]
    gcw[...] = pack[0:KERNEL, :]
    gcb[...] = pack[KERNEL : KERNEL + 1, :].reshape(width)
    gscale[...] = pack[8:12, :]
    gshift[...] = pack[12:16, :]
    gls[...] = pack[16:17, :].reshape(width)
    gdb[...] = pack[17:18, :].reshape(width)
    rows = [pack[18 + i : 19 + i, :] for i in range(6)]
    ghb[...] = jnp.concatenate(rows[:3], 1)[:, : ghb.shape[0]].reshape(ghb.shape[0])
    gub[...] = jnp.concatenate(rows[3:], 1).reshape(gub.shape[0])


def edges(value, index):
    n = value.shape[1]
    return jnp.where(index == 0, value[:, n - 8 :], value[:, :8])


def to_chunks(wave):
    clips, samples = wave.shape
    return wave.reshape(clips, samples // LANES, LANES).transpose(1, 0, 2).reshape(-1, LANES)


def from_chunks(chunks, clips):
    rows = chunks.shape[0] // clips
    return chunks.reshape(rows, clips, LANES).transpose(1, 0, 2).reshape(clips, rows * LANES)


def body(
    inputs,
    band_ids,
    offsets,
    conv_weight,
    conv_bias,
    scale_table,
    shift_table,
    up_weight,
    up_bias,
    down_weight,
    down_bias,
    layer_scale,
    head_weight,
    head_bias,
    wave_cotangent,
):
    clips, frames, width = inputs.shape
    assert lax.axis_size("tm") == 2
    nfft = head_weight.shape[1] - 2
    half = nfft // 2
    hidden = up_weight.shape[1]
    tm = lax.axis_index("tm")
    core = lax.axis_index("clip") % 2
    swap = lambda v: lax.ppermute(v, "tm", [(0, 1), (1, 0)])
    transforms, windows, inverse, turns = tables(nfft)
    dft = [jnp.asarray(v) for pair in transforms for v in pair]
    consts = dft + [jnp.asarray(windows), jnp.asarray(inverse)]

    edge = swap(edges(inputs, tm))
    cot_edge = swap(jnp.pad(wave_cotangent[:, :nfft].reshape(clips, 2, half), ((0, 0), (0, 6), (0, 0))))
    weights = (
        conv_weight,
        conv_bias,
        scale_table,
        shift_table,
        up_weight,
        up_bias,
        down_weight,
        down_bias,
        layer_scale,
        head_weight.T,
        head_bias,
    )
    (
        norm, istd, adt_h, adt_l, act_h, act_l, slope, spec, gm, gb_h, gb_l, gbt_h, gbt_l, hg_keep, hg_send, small,
    ) = run_head(
        band_ids, offsets, inputs, edge, to_chunks(wave_cotangent), cot_edge, weights, jnp.asarray(turns), consts
    )

    sums = Sums()
    turn = 0
    totals = [sums.add(halves_steps(hg_keep, hg_send, turn), {5: 2})]
    blks = frames // ROWS
    carry = jnp.zeros((clips, 8, half), F32)
    gubs, gus = [], []
    for size, part in FFN_PARTS:
        results = run_ffn(
            (gb_h, gb_l), (gbt_h, gbt_l), (act_h, act_l), slope, (adt_h, adt_l), down_weight, size, part,
            waits=sums.waits(),
        )
        keep, send, gub, gu_h, gu_l = sums.advance(results)
        turn += 1
        totals.append(sums.add(halves_steps(keep, send, turn), {3: 2} if turn == 1 else {}))
        gubs.append(gub)
        gus.append((gu_h, gu_l))
    normed = []
    for clip in range(clips):
        results = run_norm(band_ids, gus, up_weight, norm, istd, scale_table, clips, clip, waits=sums.waits())
        normed.append(sums.advance(results))
    gh = [v[0][None] for v in normed]
    gh_edge = swap(jnp.concatenate([edges(v, tm) for v in gh]))
    wave, carry = run_wave(offsets, spec, consts, clips, 0, blks // 2, carry, waits=sums.waits())
    wave, carry = sums.advance((wave, carry))
    so_far = (None, jnp.zeros((8 * (KERNEL + 1), width), F32))
    gm = gm.reshape(clips, frames, width)
    for clip in range(clips):
        so_far = run_conv(
            offsets, inputs, edge, gh[clip], gh_edge, gm, conv_weight, clip, so_far, waits=sums.waits()
        )
        so_far = sums.advance(so_far)
    grad_inputs, acc = so_far
    pack = pl.pallas_call(pack_kernel, out_shape=SDS((32, width), F32), name="pack")(
        acc, small, *[v[1] for v in normed], *[v[2] for v in normed], *gubs
    )
    totals.append(sums.add(whole_steps(pack)))

    wave, tail = run_wave(
        offsets, spec, consts, clips, blks // 2, blks - blks // 2, carry, wave, waits=sums.waits()
    )
    wave, tail = sums.advance((wave, tail))
    arrived = lax.ppermute(tail[:, :2].reshape(clips, nfft), "tm", [(0, 1)])
    arrived = arrived * jnp.tile(jnp.asarray(inverse[3:4]), (1, 2))
    wave = wave.at[: clips * nfft // LANES].add(to_chunks(arrived))
    waveform = from_chunks(wave, clips)

    head_total, *ffn_totals, small_total = totals
    head_grad = order_head(sums.finish(head_total), nfft + 2, sums.waits())
    head_grad = sums.advance(head_grad)
    ffn_grads = ()
    for (_, part), total in zip(FFN_PARTS, ffn_totals):
        total = sums.finish(total)
        ffn_grads = order_ffn(total, hidden, part, ffn_grads, sums.waits())
        ffn_grads = sums.advance(ffn_grads)
    down_grad, up_grad = ffn_grads
    pack = sums.finish(small_total)
    small_shapes = [(KERNEL, width), (width,), scale_table.shape, scale_table.shape]
    small_shapes += [(width,), (width,), (nfft + 2,), (hidden,)]
    gcw, gcb, gscale, gshift, gls, gdb, ghb, gub = pl.pallas_call(
        unpack_kernel, out_shape=[SDS(shape, F32) for shape in small_shapes], name="unpack"
    )(pack)
    return (
        waveform,
        grad_inputs,
        gcw,
        gcb,
        gscale,
        gshift,
        up_grad,
        gub,
        down_grad,
        gdb,
        gls,
        head_grad.T,
        ghb,
    )


def solution(mesh):
    in_specs = (P("clip", "tm", None), P("clip"), P("clip")) + (P(),) * 11 + (P("clip", "tm"),)
    out_specs = (P("clip", "tm"), P("clip", "tm", None)) + (P(),) * 11
    return jax.shard_map(body, mesh=mesh, in_specs=in_specs, out_specs=out_specs, check_vma=False)
```

time: 403 us -> 340 us (0.84)
  blocking collectives: 42.1 us -> 0 us
  waiting for transfers between devices: 83.9 us -> 49.4 us
  starting transfers between devices: 14.5 us -> 36.6 us
  matrix products: 19.6 us -> 0 us
  other arithmetic: 13.4 us -> 31.6 us
  Pallas kernels: 196 us -> 210 us
  between operations: 14.5 us -> 1.37 us
  local copies, waits for them, and re-layouts: 18.4 us -> 10.1 us
    psum x1 -> x0, waiting for transfers between devices: 81.6 us -> none  [body(): lax.psum((gcw, gcb, gscale, gshift, *gup, *gub, *gdn, gmb, gls, ghw, ghwe...]
    ppermute x6 -> x33, waiting for transfers between devices: 2.35 us -> 49.4 us  [the longest x29 45.5 us: exchange(): lax.ppermute(value, axis, [(i, i ^ distance) for i in range(lax.axis_size...]
    psum x1 -> x0, blocking collectives: 42.1 us -> none  [body(): lax.psum((gcw, gcb, gscale, gshift, *gup, *gub, *gdn, gmb, gls, ghw, ghwe...]
    ppermute x6 -> x33, starting transfers between devices: 14.5 us -> 36.6 us  [the longest x29 29.6 us: exchange(): lax.ppermute(value, axis, [(i, i ^ distance) for i in range(lax.axis_size...]
    add x1 -> x21, other arithmetic: 0.71 us -> 22.3 us  [the longest x6 8.18 us: halves_steps(): value = value + (yield (value, level))]
    dot_general x6 -> x0, matrix products: 19.6 us -> none  [the longest x4 15.5 us: dot(): return lax.dot_general(a, b, dims, preferred_element_type=F32)]
    pallas_call x6 -> x13, Pallas kernels: 105 us -> 124 us  [the longest x2 53.2 us: run_ffn(): pl.pallas_call(ffn_kernel, grid=(count // rows,), in_specs=in_specs + wai...]
    pallas_call x1, Pallas kernels: 90.4 us -> 85.9 us  [run_head(): pl.pallas_call(head_kernel, grid_spec=pltpu.PrefetchScalarGridSpec(num_sc...]
  transfers between devices with their start and end apart: 7 -> 33, of which waited for: 2 -> 13; matrix products, arithmetic and copies ran while one was open for 7% -> 7% of each run, Pallas kernels for 12% -> 36%
where the time goes in v2:
time: 340 us; the launch traced here: 339 us
  Pallas kernels  210 us (62%)
  waiting for transfers between devices  49.4 us (15%)
  starting transfers between devices  36.6 us (11%)
  other arithmetic  31.6 us (9%)
  local copies, waits for them, and re-layouts  10.1 us (3%)
    pallas_call x1, Pallas kernels, run_head(): pl.pallas_call(head_kernel, grid_spec=pltpu.PrefetchScalarGridSpec(num_sc...  85.9 us
    pallas_call x2, Pallas kernels, run_ffn(): pl.pallas_call(ffn_kernel, grid=(count // rows,), in_specs=in_specs + wai...  53.2 us
    ppermute x29, waiting for transfers between devices, exchange(): lax.ppermute(value, axis, [(i, i ^ distance) for i in range(lax.axis_size...  45.5 us
    ppermute x29, starting transfers between devices, exchange(): lax.ppermute(value, axis, [(i, i ^ distance) for i in range(lax.axis_size...  29.6 us
    pallas_call x2, Pallas kernels, run_norm(): pl.pallas_call(functools.partial(norm_kernel, [pair[0].shape[1] for pair...  22.9 us
    pallas_call x2, Pallas kernels, run_wave(): pl.pallas_call(functools.partial(wave_kernel, first_blk, count // clips),...  19.7 us
    pallas_call x2, Pallas kernels, run_conv(): pl.pallas_call(functools.partial(conv_kernel, clip), grid_spec=pltpu.Pref...  13.9 us
    add x6, other arithmetic, halves_steps(): value = value + (yield (value, level))  8.18 us
  transfers between devices with their start and end apart: 33, of which 13 were waited for; matrix products, arithmetic and copies ran while one was open for 7% of the time, Pallas kernels for 36%

profile of v2, /device:TPU:0, one launch (start us, length us, event | category | flops | bytes accessed | tf_op | source)
XLA Modules:
  0.0 338.7 jit_solution(936284199784993185)
XLA Ops:
  1.4 3.0 collective-permute-start.1
  5.2 3.9 %collective-permute-done.edge_ref = f32[2,8,512]{2,1,0:T(8,128)S(1)} collective-permute-done((f32[2,8,512]{2,1,0:T(8,128)S(1)}, f32[2,8,512]{2,1,0:T(8,128)S(1)}, u32[]{:S(2)}, u32[]{:S(2)}) %collective-permute-start) | collective-permute-done | bytes 32800 | tf_op jit(solution)/shard_map/ppermute | solution.py:1098
  9.7 85.9 %head.1 = (f32[2048,512]{1,0:T(8,128)}, f32[2048,128]{1,0:T(8,128)}, bf16[512,2048]{1,0:T(8,128)(2,1)}, bf16[512,2048]{1,0:T(8,128)(2,1)}, bf16[2048,1536]{1,0:T...) custom-call(s32[2]{0:T(128)} %bands.5, s32[2]{0:T(128)} %offsets.9, ...), custom_call_target="tpu_custom_call" | custom-call | flops 80000000000 | bytes 90000000 | tf_op jit(solution)/shard_map/head/pallas_call | solution.py:522
  95.7 3.3 collective-permute-done.2
  99.0 1.6 add.114
  100.7 1.6 collective-permute-start.3
  102.3 33.2 %ffn_grads.2 = (f32[1024,512]{1,0:T(8,128)}, f32[1024,512]{1,0:T(8,128)}, f32[1,1024]{1,0:T(1,128)}, bf16[2048,1024]{1,0:T(8,128)(2,1)}, bf16[2048,1024]{1,0:T(8,128)(2,1)}) custom-call(bf16[2048,512]{1,0:T(8,128)(2,1)} %get-tuple-element.130.gb_h, bf16[2048,512]{1,0:T(8,128)(2,1)} %get-tuple-element.131.gb_l, bf16[512,2048]{1,0:T(8,128)(2,1)} %get-tuple-element.132.gbt_h, ...), custom_call_target="tpu_custom_call" | custom-call | flops 19327352832 | bytes 25165824 | tf_op jit(solution)/shard_map/ffn_grads/pallas_call | solution.py:586
  136.4 3.7 %collective-permute-done.4 = f32[1024,512]{1,0:T(8,128)} collective-permute-done((f32[1024,512]{1,0:T(8,128)}, f32[1024,512]{1,0:T(8,128)}, u32[]{:S(2)}, u32[]{:S(2)}) %collective-permute-start.4) | collective-permute-done | bytes 2097184 | tf_op jit(solution)/shard_map/ppermute | solution.py:893
  140.1 2.7 add.117
  145.4 1.6 collective-permute-start.5
  147.0 20.0 %ffn_grads.3 = (f32[512,512]{1,0:T(8,128)}, f32[512,512]{1,0:T(8,128)}, f32[1,512]{1,0:T(1,128)}, bf16[2048,512]{1,0:T(8,128)(2,1)}, bf16[2048,512]{1,0:T(8,128)(2,1)}) custom-call(bf16[2048,512]{1,0:T(8,128)(2,1)} %get-tuple-element.130.gb_h, bf16[2048,512]{1,0:T(8,128)(2,1)} %get-tuple-element.131.gb_l, bf16[512,2048]{1,0:T(8,128)(2,1)} %get-tuple-element.132.gbt_h, ...), custom_call_target="tpu_custom_call" | custom-call | flops 9663676416 | bytes 12582912 | tf_op jit(solution)/shard_map/ffn_grads/pallas_call | solution.py:586
  167.0 9.6 %collective-permute-done.5 = f32[168,512]{1,0:T(8,128)S(1)} collective-permute-done((f32[168,512]{1,0:T(8,128)S(1)}, f32[168,512]{1,0:T(8,128)S(1)}, u32[]{:S(2)}, u32[]{:S(2)}) %collective-permute-start.5) | collective-permute-done | bytes 344096 | tf_op jit(solution)/shard_map/ppermute | solution.py:893
  177.4 1.5 dynamic-slice_add_fusion
  180.4 1.4 add.129
  183.6 1.5 collective-permute-start.7
  185.1 11.4 %norm_grads.2 = (f32[1024,512]{1,0:T(8,128)}, f32[4,512]{1,0:T(4,128)}, f32[4,512]{1,0:T(4,128)}) custom-call(s32[2]{0:T(128)} %bands.5, bf16[2048,1024]{1,0:T(8,128)(2,1)} %get-tuple-element.156.refs_0_, bf16[2048,1024]{1,0:T(8,128)(2,1)} %get-tuple-element.157.refs_1_, bf16[2048,512]{1,0:T(8,128)(2,1)} %get-tuple-element.158.refs_2_, ...), custom_call_target="tpu_custom_call" | custom-call | flops 5000000000 | bytes 12000000 | tf_op jit(solution)/shard_map/norm_grads/pallas_call | solution.py:664
  196.5 8.2 %collective-permute-done.10 = f32[256,512]{1,0:T(8,128)} collective-permute-done((f32[256,512]{1,0:T(8,128)S(1)}, f32[256,512]{1,0:T(8,128)}, u32[]{:S(2)}, u32[]{:S(2)}) %collective-permute-start.10) | collective-permute-done | bytes 524320 | tf_op jit(solution)/shard_map/ppermute | solution.py:893
  207.8 1.6 collective-permute-start.12
  209.4 2.6 collective-permute-start.11
  212.0 11.4 %norm_grads.3 = (f32[1024,512]{1,0:T(8,128)}, f32[4,512]{1,0:T(4,128)}, f32[4,512]{1,0:T(4,128)}) custom-call(s32[2]{0:T(128)} %bands.5, bf16[2048,1024]{1,0:T(8,128)(2,1)} %get-tuple-element.156.refs_0_, bf16[2048,1024]{1,0:T(8,128)(2,1)} %get-tuple-element.157.refs_1_, bf16[2048,512]{1,0:T(8,128)(2,1)} %get-tuple-element.158.refs_2_, ...), custom_call_target="tpu_custom_call" | custom-call | flops 5000000000 | bytes 12000000 | tf_op jit(solution)/shard_map/norm_grads/pallas_call | solution.py:664
  224.2 3.4 %collective-permute-done.11 = f32[168,512]{1,0:T(8,128)S(1)} collective-permute-done((f32[168,512]{1,0:T(8,128)S(1)}, f32[168,512]{1,0:T(8,128)S(1)}, u32[]{:S(2)}, u32[]{:S(2)}) %collective-permute-start.11) | collective-permute-done | bytes 344096 | tf_op jit(solution)/shard_map/ppermute | solution.py:893
  229.2 1.6 collective-permute-start.18
  230.8 1.9 add.134.refs_1_
  233.8 2.6 collective-permute-start.16
  236.9 1.6 collective-permute-start.14
  239.2 9.8 %wave.2 = (f32[5120,128]{1,0:T(8,128)}, f32[2,8,640]{2,1,0:T(8,128)}) custom-call(s32[2]{0:T(128)} %offsets.9, f32[2048,1280]{1,0:T(8,128)} %get-tuple-element.174.spec, f32[2,8,640]{2,1,0:T(8,128)} %broadcast_in_dim.12.carry, bf16[512,512]{1,0:T(8,128)(2,1)} %constant.127.clone.t1h, bf16[512,512]{1,0:T(8,128)(2,1)} %constant.128.clone.t1l, ...), custom_call_target="tpu_custom_call" | custom-call | flops 5000000000 | bytes 8000000 | tf_op jit(solution)/shard_map/wave/pallas_call | solution.py:865
  252.0 1.4 collective-permute-start.17
  254.9 6.9 %conv_grads.2 = (f32[2,1024,512]{2,1,0:T(8,128)}, f32[64,512]{1,0:T(8,128)}) custom-call(s32[2]{0:T(128)} %offsets.9, f32[2,1024,512]{2,1,0:T(8,128)} %x_down.5, f32[2,1024,512]{2,1,0:T(8,128)} %x_down.5, f32[2,1024,512]{2,1,0:T(8,128)} %x_down.5, f32[2,8,512]{2,1,0:T(8,128)} %copy-done.36, f32[1,1024,512]{2,1,0:T(8,128)} %bitcast.20, ...), custom_call_target="tpu_custom_call" | custom-call | flops 5000000000 | bytes 17000000 | tf_op jit(solution)/shard_map/conv_grads/pallas_call | solution.py:752
  261.8 7.3 %collective-permute-done.14 = f32[256,512]{1,0:T(8,128)S(1)} collective-permute-done((f32[256,512]{1,0:T(8,128)}, f32[256,512]{1,0:T(8,128)S(1)}, u32[]{:S(2)}, u32[]{:S(2)}) %collective-permute-start.14) | collective-permute-done | bytes 524320 | tf_op jit(solution)/shard_map/ppermute | solution.py:893
  269.0 3.1 collective-permute-done.17
  274.1 1.7 add.140.refs_2_
  275.8 1.5 collective-permute-start.21
  277.3 7.0 %conv_grads.3 = (f32[2,1024,512]{2,1,0:T(8,128)}, f32[64,512]{1,0:T(8,128)}) custom-call(s32[2]{0:T(128)} %offsets.9, f32[2,1024,512]{2,1,0:T(8,128)} %x_down.5, f32[2,1024,512]{2,1,0:T(8,128)} %x_down.5, f32[2,1024,512]{2,1,0:T(8,128)} %x_down.5, f32[2,8,512]{2,1,0:T(8,128)} %copy-done.36, ...), custom_call_target="tpu_custom_call", output_to_operand_aliasing={{0}: (12, {})} | custom-call | flops 5000000000 | bytes 17000000 | tf_op jit(solution)/shard_map/conv_grads/pallas_call | solution.py:752
  285.8 2.0 collective-permute-start.22
  287.8 1.6 pack.1
  293.5 9.9 %wave.3 = (f32[5120,128]{1,0:T(8,128)}, f32[2,8,640]{2,1,0:T(8,128)}) custom-call(s32[2]{0:T(128)} %offsets.9, f32[2048,1280]{1,0:T(8,128)} %get-tuple-element.174.spec, f32[2,8,640]{2,1,0:T(8,128)} %get-tuple-element.200.carry, bf16[512,512]{1,0:T(8,128)(2,1)} %constant.127.clone.t1h, ...), custom_call_target="tpu_custom_call", output_to_operand_aliasing={{0}: (11, {})} | custom-call | flops 5000000000 | bytes 8000000 | tf_op jit(solution)/shard_map/wave/pallas_call | solution.py:865
  303.4 2.9 collective-permute-done.25
  306.3 2.2 collective-permute-done.22
  308.5 1.5 pad_maximum_fusion.mine
  311.2 2.2 pad_maximum_fusion.3.mine
  313.5 1.7 collective-permute-start.27
  315.9 2.3 collective-permute-start.26
  318.3 3.4 %head_order.1 = f32[1282,512]{1,0:T(8,128)} custom-call(f32[672,512]{1,0:T(8,128)} %copy-done.3, f32[672,512]{1,0:T(8,128)} %collective-permute-done.28.other, f32[32,512]{1,0:T(8,128)} %copy-done.30), custom_call_target="tpu_custom_call" | custom-call | tf_op jit(solution)/shard_map/head_order/pallas_call | solution.py:1016
  323.2 4.5 %ffn_order.2 = (f32[1536,512]{1,0:T(8,128)}, f32[512,1536]{1,0:T(8,128)}) custom-call(f32[1024,512]{1,0:T(8,128)} %copy-done.2, f32[1024,512]{1,0:T(8,128)} %collective-permute-done.30.other, f32[32,512]{1,0:T(8,128)} %copy-done.28), custom_call_target="tpu_custom_call" | custom-call | tf_op jit(solution)/shard_map/ffn_order/pallas_call | solution.py:1030
  328.6 2.1 collective-permute-start.31
  332.7 3.0 ffn_order.3
  335.7 1.5 add.146.pack
  337.2 1.5 unpack.1
  (159 shorter events, 35.1 us)
Async XLA Ops:
  1.4 7.7 %collective-permute-start.1 = (f32[2,8,640]{2,1,0:T(8,128)S(1)}, f32[2,8,640]{2,1,0:T(8,128)S(1)}, u32[]{:S(2)}, u32[]{:S(2)}) collective-permute-start(f32[2,8,640]{2,1,0:T(8,128)S(1)} %pad.6), channel_id=1, source_target_pairs={{0,1},{1,0},{2,3},{3,2},{4,5},{5,4},{6,7},{7,6},{8,9},{9,8},{10,11... | collective-permute-start | bytes 122888 | tf_op jit(solution)/shard_map/ppermute | solution.py:1098
  5.2 3.9 %collective-permute-start = (f32[2,8,512]{2,1,0:T(8,128)S(1)}, f32[2,8,512]{2,1,0:T(8,128)S(1)}, u32[]{:S(2)}, u32[]{:S(2)}) collective-permute-start(f32[2,8,512]{2,1,0:T(8,128)S(1)} %slice_select_fusion), channel_id=1, source_target_pairs={{0,1},{1,0},{2,3},{3,2},{4,5},{5,4},{6,7},{7,6},{8,9},{9,8},{10,11... | collective-permute-start | bytes 98312 | tf_op jit(solution)/shard_map/ppermute | solution.py:1098
  95.6 3.4 %collective-permute-start.2 = (f32[672,512]{1,0:T(8,128)}, f32[672,512]{1,0:T(8,128)S(1)}, u32[]{:S(2)}, u32[]{:S(2)}) collective-permute-start(f32[672,512]{1,0:T(8,128)} %get-tuple-element.129), channel_id=1, source_target_pairs={{0,2},{2,0},{4,6},{6,4},{8,10},{10,8},{12,14},{14,12},{16,18},{18,... | collective-permute-start | bytes 4128776 | tf_op jit(solution)/shard_map/ppermute | solution.py:893
  100.7 34.8 %collective-permute-start.3 = (f32[336,512]{1,0:T(8,128)S(1)}, f32[336,512]{1,0:T(8,128)S(1)}, u32[]{:S(2)}, u32[]{:S(2)}) collective-permute-start(f32[336,512]{1,0:T(8,128)S(1)} %constant_dynamic-slice_fusion.5.refs_0_), channel_id=1, source_target_pairs={{0,4},{2,6},{4,0},{6,2},{8,12},{10,14},{12,8},{14,10},{16,20},{18,... | collective-permute-start | bytes 2064392 | tf_op jit(solution)/shard_map/ppermute | solution.py:893
  135.5 4.6 %collective-permute-start.4 = (f32[1024,512]{1,0:T(8,128)}, f32[1024,512]{1,0:T(8,128)}, u32[]{:S(2)}, u32[]{:S(2)}) collective-permute-start(f32[1024,512]{1,0:T(8,128)} %get-tuple-element.145), channel_id=1, source_target_pairs={{0,2},{2,0},{4,6},{6,4},{8,10},{10,8},{12,14},{14,12},{16,18},{18,... | collective-permute-start | bytes 6291464 | tf_op jit(solution)/shard_map/ppermute | solution.py:893
  143.9 33.5 %collective-permute-start.6 = (f32[512,512]{1,0:T(8,128)}, f32[512,512]{1,0:T(8,128)}, u32[]{:S(2)}, u32[]{:S(2)}) collective-permute-start(f32[512,512]{1,0:T(8,128)} %constant_dynamic-slice_fusion.3.refs_1_), channel_id=1, source_target_pairs={{0,1},{1,0},{2,3},{3,2},{4,5},{5,4},{6,7},{7,6},{8,9},{9,8},{10,11... | collective-permute-start | bytes 3145736 | tf_op jit(solution)/shard_map/ppermute | solution.py:893
  145.4 31.3 %collective-permute-start.5 = (f32[168,512]{1,0:T(8,128)S(1)}, f32[168,512]{1,0:T(8,128)S(1)}, u32[]{:S(2)}, u32[]{:S(2)}) collective-permute-start(f32[168,512]{1,0:T(8,128)S(1)} %constant_dynamic-slice_fusion.4.refs_0_), channel_id=1, source_target_pairs={{0,1},{1,0},{2,3},{3,2},{4,5},{5,4},{6,7},{7,6},{8,9},{9,8},{10,11... | collective-permute-start | bytes 1032200 | tf_op jit(solution)/shard_map/ppermute | solution.py:893
  177.4 3.0 collective-permute-start.9
  179.0 3.8 %copy-start.10 = (f32[336,512]{1,0:T(8,128)S(1)}, f32[336,512]{1,0:T(8,128)}, u32[]{:S(2)}) copy-start(f32[336,512]{1,0:T(8,128)} %copy-done.9) | copy-start | bytes 2064388
  179.0 17.5 %collective-permute-start.8 = (f32[256,512]{1,0:T(8,128)S(1)}, f32[256,512]{1,0:T(8,128)S(1)}, u32[]{:S(2)}, u32[]{:S(2)}) collective-permute-start(f32[256,512]{1,0:T(8,128)S(1)} %constant_dynamic-slice_fusion.2.refs_9_), channel_id=1, source_target_pairs={{0,4},{2,6},{4,0},{6,2},{8,12},{10,14},{12,8},{14,10},{16,20},{18,... | collective-permute-start | bytes 1572872 | tf_op jit(solution)/shard_map/ppermute | solution.py:893
  181.9 22.8 %collective-permute-start.10 = (f32[256,512]{1,0:T(8,128)S(1)}, f32[256,512]{1,0:T(8,128)}, u32[]{:S(2)}, u32[]{:S(2)}) collective-permute-start(f32[256,512]{1,0:T(8,128)S(1)} %constant_dynamic-slice_fusion.1.refs_10_), channel_id=1, source_target_pairs={{0,4},{2,6},{4,0},{6,2},{8,12},{10,14},{12,8},{14,10},{16,20},{18,... | collective-permute-start | bytes 1572872 | tf_op jit(solution)/shard_map/ppermute | solution.py:893
  183.6 13.0 %collective-permute-start.7 = (f32[168,512]{1,0:T(8,128)}, f32[168,512]{1,0:T(8,128)S(1)}, u32[]{:S(2)}, u32[]{:S(2)}) collective-permute-start(f32[168,512]{1,0:T(8,128)} %dynamic-slice_add_fusion.4.refs_8_), channel_id=1, source_target_pairs={{0,8},{2,10},{4,12},{6,14},{8,0},{10,2},{12,4},{14,6},{16,24},{18,... | collective-permute-start | bytes 1032200 | tf_op jit(solution)/shard_map/ppermute | solution.py:893
  206.0 6.0 %copy-start.4 = (f32[256,512]{1,0:T(8,128)}, f32[256,512]{1,0:T(8,128)S(1)}, u32[]{:S(2)}) copy-start(f32[256,512]{1,0:T(8,128)S(1)} %dynamic-slice_add_fusion.3.refs_9_) | copy-start | bytes 1572868
  207.2 4.8 %copy-start.5 = (f32[168,512]{1,0:T(8,128)}, f32[168,512]{1,0:T(8,128)S(1)}, u32[]{:S(2)}) copy-start(f32[168,512]{1,0:T(8,128)S(1)} %add.131.refs_8_) | copy-start | bytes 1032196
  207.2 4.7 %copy-start.17 = (f32[128,512]{1,0:T(8,128)}, f32[128,512]{1,0:T(8,128)S(1)}, u32[]{:S(2)}) copy-start(f32[128,512]{1,0:T(8,128)S(1)} %constant_dynamic-slice_fusion.refs_10_) | copy-start | bytes 786436
  207.3 16.9 %collective-permute-start.13 = (f32[128,512]{1,0:T(8,128)S(1)}, f32[128,512]{1,0:T(8,128)S(1)}, u32[]{:S(2)}, u32[]{:S(2)}) collective-permute-start(f32[128,512]{1,0:T(8,128)S(1)} %constant_dynamic-slice_fusion.refs_10_), channel_id=1, source_target_pairs={{0,1},{1,0},{2,3},{3,2},{4,5},{5,4},{6,7},{7,6},{8,9},{9,8},{10,11... | collective-permute-start | bytes 786440 | tf_op jit(solution)/shard_map/ppermute | solution.py:893
  207.8 20.6 %collective-permute-start.12 = (f32[256,512]{1,0:T(8,128)S(1)}, f32[256,512]{1,0:T(8,128)S(1)}, u32[]{:S(2)}, u32[]{:S(2)}) collective-permute-start(f32[256,512]{1,0:T(8,128)S(1)} %dynamic-slice_add_fusion.3.refs_9_), channel_id=1, source_target_pairs={{0,8},{2,10},{4,12},{6,14},{8,0},{10,2},{12,4},{14,6},{16,24},{18,... | collective-permute-start | bytes 1572872 | tf_op jit(solution)/shard_map/ppermute | solution.py:893
  209.4 18.2 %collective-permute-start.11 = (f32[168,512]{1,0:T(8,128)S(1)}, f32[168,512]{1,0:T(8,128)S(1)}, u32[]{:S(2)}, u32[]{:S(2)}) collective-permute-start(f32[168,512]{1,0:T(8,128)S(1)} %add.131.refs_8_), channel_id=1, source_target_pairs={{0,16},{2,18},{4,20},{6,22},{8,24},{10,26},{12,28},{14,30},{16,0},... | collective-permute-start | bytes 1032200 | tf_op jit(solution)/shard_map/ppermute | solution.py:893
  229.2 25.0 %collective-permute-start.18 = (f32[2,8,512]{2,1,0:T(8,128)S(1)}, f32[2,8,512]{2,1,0:T(8,128)S(1)}, u32[]{:S(2)}, u32[]{:S(2)}) collective-permute-start(f32[2,8,512]{2,1,0:T(8,128)S(1)} %pad_maximum_fusion.6), channel_id=1, source_target_pairs={{0,1},{1,0},{2,3},{3,2},{4,5},{5,4},{6,7},{7,6},{8,9},{9,8},{10,11... | collective-permute-start | bytes 98312 | tf_op jit(solution)/shard_map/ppermute | solution.py:1098
  233.7 5.4 %copy-start.6 = (f32[168,512]{1,0:T(8,128)}, f32[168,512]{1,0:T(8,128)S(1)}, u32[]{:S(2)}) copy-start(f32[168,512]{1,0:T(8,128)S(1)} %add.137.refs_0_) | copy-start | bytes 1032196
  233.8 5.4 %copy-start.20 = (f32[128,512]{1,0:T(8,128)}, f32[128,512]{1,0:T(8,128)S(1)}, u32[]{:S(2)}) copy-start(f32[128,512]{1,0:T(8,128)S(1)} %dynamic-slice_add_fusion.5.refs_2_) | copy-start | bytes 786436
  233.8 15.2 %collective-permute-start.16 = (f32[128,512]{1,0:T(8,128)S(1)}, f32[128,512]{1,0:T(8,128)S(1)}, u32[]{:S(2)}, u32[]{:S(2)}) collective-permute-start(f32[128,512]{1,0:T(8,128)S(1)} %dynamic-slice_add_fusion.5.refs_2_), channel_id=1, source_target_pairs={{0,8},{2,10},{4,12},{6,14},{8,0},{10,2},{12,4},{14,6},{16,24},{18,... | collective-permute-start | bytes 786440 | tf_op jit(solution)/shard_map/ppermute | solution.py:893
  236.4 12.6 %collective-permute-start.15 = (f32[168,512]{1,0:T(8,128)S(1)}, f32[168,512]{1,0:T(8,128)S(1)}, u32[]{:S(2)}, u32[]{:S(2)}) collective-permute-start(f32[168,512]{1,0:T(8,128)S(1)} %add.137.refs_0_), channel_id=1, source_target_pairs={{0,1},{1,0},{2,3},{3,2},{4,5},{5,4},{6,7},{7,6},{8,9},{9,8},{10,11... | collective-permute-start | bytes 1032200 | tf_op jit(solution)/shard_map/ppermute | solution.py:893
  236.9 32.1 %collective-permute-start.14 = (f32[256,512]{1,0:T(8,128)}, f32[256,512]{1,0:T(8,128)S(1)}, u32[]{:S(2)}, u32[]{:S(2)}) collective-permute-start(f32[256,512]{1,0:T(8,128)} %add.134.refs_1_), channel_id=1, source_target_pairs={{0,16},{2,18},{4,20},{6,22},{8,24},{10,26},{12,28},{14,30},{16,0},... | collective-permute-start | bytes 1572872 | tf_op jit(solution)/shard_map/ppermute | solution.py:893
  250.8 4.1 %copy-start.8 = (f32[336,512]{1,0:T(8,128)}, f32[336,512]{1,0:T(8,128)S(1)}, u32[]{:S(2)}) copy-start(f32[336,512]{1,0:T(8,128)S(1)} %pad_maximum_fusion.4.refs_0_) | copy-start | bytes 2064388
  252.0 20.1 %collective-permute-start.17 = (f32[128,512]{1,0:T(8,128)S(1)}, f32[128,512]{1,0:T(8,128)S(1)}, u32[]{:S(2)}, u32[]{:S(2)}) collective-permute-start(f32[128,512]{1,0:T(8,128)S(1)} %add.138.refs_1_), channel_id=1, source_target_pairs={{0,16},{2,18},{4,20},{6,22},{8,24},{10,26},{12,28},{14,30},{16,0},... | collective-permute-start | bytes 786440 | tf_op jit(solution)/shard_map/ppermute | solution.py:893
  253.4 30.9 %collective-permute-start.19 = (f32[336,512]{1,0:T(8,128)S(1)}, f32[336,512]{1,0:T(8,128)S(1)}, u32[]{:S(2)}, u32[]{:S(2)}) collective-permute-start(f32[336,512]{1,0:T(8,128)S(1)} %pad_maximum_fusion.4.refs_0_), channel_id=1, source_target_pairs={{0,4},{2,6},{4,0},{6,2},{8,12},{10,14},{12,8},{14,10},{16,20},{18,... | collective-permute-start | bytes 2064392 | tf_op jit(solution)/shard_map/ppermute | solution.py:893
  273.2 4.1 %copy-start = (f32[256,512]{1,0:T(8,128)}, f32[256,512]{1,0:T(8,128)S(1)}, u32[]{:S(2)}) copy-start(f32[256,512]{1,0:T(8,128)S(1)} %add.139.refs_1_) | copy-start | bytes 1572868
  273.2 11.4 %collective-permute-start.20 = (f32[256,512]{1,0:T(8,128)S(1)}, f32[256,512]{1,0:T(8,128)S(1)}, u32[]{:S(2)}, u32[]{:S(2)}) collective-permute-start(f32[256,512]{1,0:T(8,128)S(1)} %add.139.refs_1_), channel_id=1, source_target_pairs={{0,4},{2,6},{4,0},{6,2},{8,12},{10,14},{12,8},{14,10},{16,20},{18,... | collective-permute-start | bytes 1572872 | tf_op jit(solution)/shard_map/ppermute | solution.py:893
  275.8 8.5 %collective-permute-start.21 = (f32[128,512]{1,0:T(8,128)}, f32[128,512]{1,0:T(8,128)S(1)}, u32[]{:S(2)}, u32[]{:S(2)}) collective-permute-start(f32[128,512]{1,0:T(8,128)} %add.140.refs_2_), channel_id=1, source_target_pairs={{0,1},{1,0},{2,3},{3,2},{4,5},{5,4},{6,7},{7,6},{8,9},{9,8},{10,11... | collective-permute-start | bytes 786440 | tf_op jit(solution)/shard_map/ppermute | solution.py:893
  284.3 19.0 %copy-start.21 = (f32[128,512]{1,0:T(8,128)}, f32[128,512]{1,0:T(8,128)S(1)}, u32[]{:S(2)}) copy-start(f32[128,512]{1,0:T(8,128)S(1)} %collective-permute-done.21) | copy-start | bytes 786436
  284.3 19.0 %copy-start.23 = (f32[336,512]{1,0:T(8,128)}, f32[336,512]{1,0:T(8,128)S(1)}, u32[]{:S(2)}) copy-start(f32[336,512]{1,0:T(8,128)S(1)} %collective-permute-done.19) | copy-start | bytes 2064388
  285.8 7.7 %copy-start.19 = (f32[512,512]{1,0:T(8,128)}, f32[512,512]{1,0:T(8,128)S(1)}, u32[]{:S(2)}) copy-start(f32[512,512]{1,0:T(8,128)S(1)} %pad_maximum_fusion.2.refs_1_) | copy-start | bytes 3145732
  285.8 22.7 %collective-permute-start.22 = (f32[512,512]{1,0:T(8,128)S(1)}, f32[512,512]{1,0:T(8,128)}, u32[]{:S(2)}, u32[]{:S(2)}) collective-permute-start(f32[512,512]{1,0:T(8,128)S(1)} %pad_maximum_fusion.2.refs_1_), channel_id=1, source_target_pairs={{0,1},{1,0},{2,3},{3,2},{4,5},{5,4},{6,7},{7,6},{8,9},{9,8},{10,11... | collective-permute-start | bytes 3145736 | tf_op jit(solution)/shard_map/ppermute | solution.py:893
  289.5 1.9 collective-permute-start.24
  290.5 15.8 %collective-permute-start.23 = (f32[256,512]{1,0:T(8,128)S(1)}, f32[256,512]{1,0:T(8,128)}, u32[]{:S(2)}, u32[]{:S(2)}) collective-permute-start(f32[256,512]{1,0:T(8,128)S(1)} %pad_maximum_fusion.5.refs_2_), channel_id=1, source_target_pairs={{0,4},{2,6},{4,0},{6,2},{8,12},{10,14},{12,8},{14,10},{16,20},{18,... | collective-permute-start | bytes 1572872 | tf_op jit(solution)/shard_map/ppermute | solution.py:893
  292.2 16.3 %copy-start.1 = (f32[256,512]{1,0:T(8,128)S(1)}, f32[256,512]{1,0:T(8,128)}, u32[]{:S(2)}) copy-start(f32[256,512]{1,0:T(8,128)} %copy-done) | copy-start | bytes 1572868
  292.2 14.1 %collective-permute-start.25 = (f32[32,512]{1,0:T(8,128)S(1)}, f32[32,512]{1,0:T(8,128)S(1)}, u32[]{:S(2)}, u32[]{:S(2)}) collective-permute-start(f32[32,512]{1,0:T(8,128)S(1)} %add.141.refs_3_), channel_id=1, source_target_pairs={{0,4},{2,6},{4,0},{6,2},{8,12},{10,14},{12,8},{14,10},{16,20},{18,... | collective-permute-start | bytes 196616 | tf_op jit(solution)/shard_map/ppermute | solution.py:893
  310.1 12.7 %collective-permute-start.30 = (f32[1024,512]{1,0:T(8,128)S(1)}, f32[1024,512]{1,0:T(8,128)}, u32[]{:S(2)}, u32[]{:S(2)}) collective-permute-start(f32[1024,512]{1,0:T(8,128)S(1)} %pad_maximum_fusion.mine), channel_id=1, source_target_pairs={{0,2},{2,0},{4,6},{6,4},{8,10},{10,8},{12,14},{14,12},{16,18},{18,... | collective-permute-start | bytes 6291464 | tf_op jit(solution)/shard_map/ppermute | solution.py:893
  310.3 8.0 %copy-start.3 = (f32[672,512]{1,0:T(8,128)}, f32[672,512]{1,0:T(8,128)S(1)}, u32[]{:S(2)}) copy-start(f32[672,512]{1,0:T(8,128)S(1)} %pad_maximum_fusion.1.mine) | copy-start | bytes 4128772
  310.3 8.0 %collective-permute-start.28 = (f32[672,512]{1,0:T(8,128)S(1)}, f32[672,512]{1,0:T(8,128)}, u32[]{:S(2)}, u32[]{:S(2)}) collective-permute-start(f32[672,512]{1,0:T(8,128)S(1)} %pad_maximum_fusion.1.mine), channel_id=1, source_target_pairs={{0,2},{2,0},{4,6},{6,4},{8,10},{10,8},{12,14},{14,12},{16,18},{18,... | collective-permute-start | bytes 4128776 | tf_op jit(solution)/shard_map/ppermute | solution.py:893
  313.5 19.3 %collective-permute-start.32 = (f32[512,512]{1,0:T(8,128)}, f32[512,512]{1,0:T(8,128)}, u32[]{:S(2)}, u32[]{:S(2)}) collective-permute-start(f32[512,512]{1,0:T(8,128)} %pad_maximum_fusion.3.mine), channel_id=1, source_target_pairs={{0,2},{2,0},{4,6},{6,4},{8,10},{10,8},{12,14},{14,12},{16,18},{18,... | collective-permute-start | bytes 3145736 | tf_op jit(solution)/shard_map/ppermute | solution.py:893
  313.5 4.8 %copy-start.30 = (f32[32,512]{1,0:T(8,128)}, f32[32,512]{1,0:T(8,128)S(1)}, u32[]{:S(2)}) copy-start(f32[32,512]{1,0:T(8,128)S(1)} %add.143.refs_0_) | copy-start | bytes 196612
  313.5 8.3 %collective-permute-start.27 = (f32[32,512]{1,0:T(8,128)S(1)}, f32[32,512]{1,0:T(8,128)S(1)}, u32[]{:S(2)}, u32[]{:S(2)}) collective-permute-start(f32[32,512]{1,0:T(8,128)S(1)} %add.143.refs_0_), channel_id=1, source_target_pairs={{0,1},{1,0},{2,3},{3,2},{4,5},{5,4},{6,7},{7,6},{8,9},{9,8},{10,11... | collective-permute-start | bytes 196616 | tf_op jit(solution)/shard_map/ppermute | solution.py:893
  315.9 6.8 %collective-permute-start.26 = (f32[2,1280]{1,0:T(2,128)S(1)}, f32[2,1280]{1,0:T(2,128)S(1)}, u32[]{:S(2)}, u32[]{:S(2)}) collective-permute-start(f32[2,1280]{1,0:T(2,128)S(1)} %bitcast.31), channel_id=1, source_target_pairs={{0,1},{2,3},{4,5},{6,7},{8,9},{10,11},{12,13},{14,15},{16,17},{18,... | collective-permute-start | bytes 30728 | tf_op jit(solution)/shard_map/ppermute | solution.py:1165
  322.6 5.1 %collective-permute-start.29 = (f32[32,512]{1,0:T(8,128)S(1)}, f32[32,512]{1,0:T(8,128)S(1)}, u32[]{:S(2)}, u32[]{:S(2)}) collective-permute-start(f32[32,512]{1,0:T(8,128)S(1)} %add.144.refs_0_), channel_id=1, source_target_pairs={{0,8},{2,10},{4,12},{6,14},{8,0},{10,2},{12,4},{14,6},{16,24},{18,... | collective-permute-start | bytes 196616 | tf_op jit(solution)/shard_map/ppermute | solution.py:893
  328.6 4.1 %copy-start.29 = (f32[32,512]{1,0:T(8,128)}, f32[32,512]{1,0:T(8,128)S(1)}, u32[]{:S(2)}) copy-start(f32[32,512]{1,0:T(8,128)S(1)} %add.145.refs_2_) | copy-start | bytes 196612
  328.6 7.1 %collective-permute-start.31 = (f32[32,512]{1,0:T(8,128)S(1)}, f32[32,512]{1,0:T(8,128)S(1)}, u32[]{:S(2)}, u32[]{:S(2)}) collective-permute-start(f32[32,512]{1,0:T(8,128)S(1)} %add.145.refs_2_), channel_id=1, source_target_pairs={{0,16},{2,18},{4,20},{6,22},{8,24},{10,26},{12,28},{14,30},{16,0},... | collective-permute-start | bytes 196616 | tf_op jit(solution)/shard_map/ppermute | solution.py:893
  (24 other events, 43.5 us)
